TPU v7x, 128 devices: a whole 4x4x4 slice. The times are simulated.
128 devices in a mesh: ctx: 8 (over x, core), vocab: 16 (over y, z).
Axes of the slice: x: 4, y: 4, z: 4, core: 2. Of those that a mesh axis runs over, the one named last changes fastest.
Arguments:
- hidden_state: bfloat16 [1024, 7168], P('ctx'), may hold values from -50 to 50
- embedded_next: bfloat16 [1024, 7168], P('ctx'), may hold values from -50 to 50
- gain_hidden: float32 [7168], replicated, may hold values from 0.1 to 1.9
- gain_embed: float32 [7168], replicated, may hold values from 0.1 to 1.9
- proj_hidden: bfloat16 [7168, 7168], P('ctx', 'vocab'), may hold values from -0.0625 to 0.0625
- proj_embed: bfloat16 [7168, 7168], P('ctx', 'vocab'), may hold values from -0.0625 to 0.0625
- final_gain: float32 [7168], P('vocab'), may hold values from 0.1 to 1.9
- head: bfloat16 [65536, 7168], P(('ctx', 'vocab')), may hold values from -0.875 to 0.875
- targets: int32 [1024], replicated, may hold values from 0 to 65535
- loss_mask: int32 [1024], replicated, may hold values 0 or 1
Outputs:
- mean_loss: float32 [], replicated
- grad_hidden: bfloat16 [1024, 7168], P('ctx', 'vocab')
- grad_embed: bfloat16 [1024, 7168], P('ctx', 'vocab')
- grad_gain_hidden: float32 [7168], P('vocab')
- grad_gain_embed: float32 [7168], P('vocab')
- grad_proj_hidden: bfloat16 [7168, 7168], P('ctx', 'vocab')
- grad_proj_embed: bfloat16 [7168, 7168], P('ctx', 'vocab')
- grad_final_gain: float32 [7168], P('vocab')
- grad_head: bfloat16 [65536, 7168], P(('ctx', 'vocab'))
All inputs are finite; a program needn't handle non-finite values.
Results may differ from a plain program's by a relative error of at most 0.023.
Values may be sent and summed in bfloat16 or wider, within the bound.
A program may use at most 256 MiB of HBM per device.

v0:
```python
import jax
import jax.numpy as jnp
from jax import lax
from jax.sharding import PartitionSpec as P

EPSILON = 1e-06


def scale_of(values):
    return lax.rsqrt(jnp.mean(values * values, axis=-1, keepdims=True) + EPSILON)


def contract_first(left, right):
    return lax.dot_general(
        left, right, (((0,), (0,)), ((), ())), preferred_element_type=jnp.float32
    )


def contract_last(left, right):
    return lax.dot_general(
        left, right, (((1,), (1,)), ((), ())), preferred_element_type=jnp.float32
    )


def local(
    hidden_state,
    embedded_next,
    gain_hidden,
    gain_embed,
    proj_hidden,
    proj_embed,
    final_gain,
    head,
    targets,
    loss_mask,
):
    model_width = hidden_state.shape[1]
    token_total = targets.shape[0]
    hidden_wide = hidden_state.astype(jnp.float32)
    embed_wide = embedded_next.astype(jnp.float32)
    hidden_scale = scale_of(hidden_wide)
    embed_scale = scale_of(embed_wide)
    normed_hidden = (hidden_wide * hidden_scale * gain_hidden).astype(jnp.bfloat16)
    normed_embed = (embed_wide * embed_scale * gain_embed).astype(jnp.bfloat16)
    hidden_cols, embed_cols = (
        lax.all_to_all(normed_hidden, "ctx", split_axis=1, concat_axis=0, tiled=True),
        lax.all_to_all(normed_embed, "ctx", split_axis=1, concat_axis=0, tiled=True),
    )
    partial_proj = jnp.dot(hidden_cols, proj_hidden, preferred_element_type=jnp.float32) + jnp.dot(
        embed_cols, proj_embed, preferred_element_type=jnp.float32
    )
    projected = lax.psum(partial_proj, "ctx")
    row_squares = lax.psum(jnp.sum(projected * projected, axis=-1), "vocab")
    row_scale = lax.rsqrt(row_squares / model_width + EPSILON)[:, None]
    normed_piece = (projected * row_scale * final_gain).astype(jnp.bfloat16)
    normed_rows = lax.all_gather(normed_piece, "vocab", axis=1, tiled=True)
    logits = contract_last(normed_rows, head)
    vocab_local = head.shape[0]
    vocab_start = (
        lax.axis_index("ctx") * lax.axis_size("vocab") + lax.axis_index("vocab")
    ) * vocab_local
    vocab_ids = vocab_start + lax.iota(jnp.int32, vocab_local)
    is_target = targets[:, None] == vocab_ids[None, :]
    exp_part = jnp.sum(jnp.exp(logits), axis=-1)
    target_part = jnp.sum(jnp.where(is_target, logits, jnp.float32(0.0)), axis=-1)
    exp_total, target_logit = lax.psum((exp_part, target_part), ("ctx", "vocab"))
    log_total = jnp.log(exp_total)
    mask_weight = loss_mask.astype(jnp.float32)
    mean_loss = jnp.sum(mask_weight * (log_total - target_logit)) / token_total
    probs = jnp.exp(logits - log_total[:, None])
    logit_grad = (mask_weight[:, None] * (probs - is_target.astype(jnp.float32))).astype(
        jnp.bfloat16
    )
    grad_head = contract_first(logit_grad, normed_rows).astype(jnp.bfloat16)
    normed_part = jnp.dot(logit_grad, head, preferred_element_type=jnp.float32)
    vocab_summed = lax.psum_scatter(
        normed_part.astype(jnp.bfloat16), "vocab", scatter_dimension=1, tiled=True
    )
    normed_grad = lax.psum(vocab_summed, "ctx").astype(jnp.float32)
    grad_final_gain = jnp.sum(normed_grad * projected * row_scale, axis=0)
    scaled_grad = normed_grad * final_gain
    row_dot = lax.psum(jnp.sum(scaled_grad * projected, axis=-1), "vocab")
    proj_grad = (
        row_scale * scaled_grad
        - projected * (row_scale * row_scale * row_scale) * (row_dot[:, None] / model_width)
    ).astype(jnp.bfloat16)
    grad_proj_hidden = contract_first(hidden_cols, proj_grad).astype(jnp.bfloat16)
    grad_proj_embed = contract_first(embed_cols, proj_grad).astype(jnp.bfloat16)
    hidden_part = contract_last(proj_grad, proj_hidden)
    embed_part = contract_last(proj_grad, proj_embed)
    hidden_tokens, embed_tokens = (
        lax.all_to_all(
            hidden_part.astype(jnp.bfloat16), "ctx", split_axis=0, concat_axis=1, tiled=True
        ).astype(hidden_part.dtype),
        lax.all_to_all(
            embed_part.astype(jnp.bfloat16), "ctx", split_axis=0, concat_axis=1, tiled=True
        ).astype(embed_part.dtype),
    )
    hidden_back, embed_back = (
        lax.psum_scatter(
            hidden_tokens.astype(jnp.bfloat16), "vocab", scatter_dimension=1, tiled=True
        ).astype(jnp.float32),
        lax.psum_scatter(
            embed_tokens.astype(jnp.bfloat16), "vocab", scatter_dimension=1, tiled=True
        ).astype(jnp.float32),
    )
    slice_width = hidden_back.shape[1]
    feature_start = lax.axis_index("vocab") * slice_width
    hidden_slice = lax.dynamic_slice_in_dim(hidden_wide, feature_start, slice_width, 1)
    embed_slice = lax.dynamic_slice_in_dim(embed_wide, feature_start, slice_width, 1)
    hidden_gain_slice = lax.dynamic_slice_in_dim(gain_hidden, feature_start, slice_width, 0)
    embed_gain_slice = lax.dynamic_slice_in_dim(gain_embed, feature_start, slice_width, 0)
    hidden_dot, embed_dot = lax.psum(
        (
            jnp.sum(hidden_back * hidden_gain_slice * hidden_slice, axis=-1),
            jnp.sum(embed_back * embed_gain_slice * embed_slice, axis=-1),
        ),
        "vocab",
    )
    grad_hidden = (
        hidden_scale * (hidden_back * hidden_gain_slice)
        - hidden_slice
        * (hidden_scale * hidden_scale * hidden_scale)
        * (hidden_dot[:, None] / model_width)
    ).astype(jnp.bfloat16)
    grad_embed = (
        embed_scale * (embed_back * embed_gain_slice)
        - embed_slice
        * (embed_scale * embed_scale * embed_scale)
        * (embed_dot[:, None] / model_width)
    ).astype(jnp.bfloat16)
    grad_gain_hidden, grad_gain_embed = lax.psum(
        (
            jnp.sum(hidden_back * hidden_slice * hidden_scale, axis=0),
            jnp.sum(embed_back * embed_slice * embed_scale, axis=0),
        ),
        "ctx",
    )
    return (
        mean_loss,
        grad_hidden,
        grad_embed,
        grad_gain_hidden,
        grad_gain_embed,
        grad_proj_hidden,
        grad_proj_embed,
        grad_final_gain,
        grad_head,
    )


def solution(mesh):
    in_specs = (
        P("ctx", None),
        P("ctx", None),
        P(),
        P(),
        P("ctx", "vocab"),
        P("ctx", "vocab"),
        P("vocab"),
        P(("ctx", "vocab"), None),
        P(),
        P(),
    )
    out_specs = (
        P(),
        P("ctx", "vocab"),
        P("ctx", "vocab"),
        P("vocab"),
        P("vocab"),
        P("ctx", "vocab"),
        P("ctx", "vocab"),
        P("vocab"),
        P(("ctx", "vocab"), None),
    )
    return jax.shard_map(local, mesh=mesh, in_specs=in_specs, out_specs=out_specs, check_vma=False)
```

profile of v0, /device:TPU:1, one launch (start us, length us, event | category | flops | bytes accessed | tf_op | source)
XLA Modules:
  0.0 827.0 jit_solution(10432507283900352977)
XLA Ops:
  7.2 3.4 copy.27
  10.6 1.0 multiply_reduce_fusion.1
  12.1 3.9 multiply_convert_fusion.1
  16.0 5.8 all-to-all-start
  21.8 3.3 copy.29
  25.2 1.0 multiply_reduce_fusion
  27.2 3.9 multiply_convert_fusion
  31.1 14.4 %all-to-all-done = bf16[128,8,896]{0,2,1:T(8,128)(2,1)} async-done(((bf16[128,8,896]{0,2,1:T(8,128)(2,1)}), bf16[128,8,896]{0,2,1:T(8,128)(2,1)}, u32[]{:S(2)}, u32[]{:S(2)}) %all-to-all-start) | async-done | bytes 1835040 | tf_op jit(solution)/shard_map/all_to_all | solution.py:46
  45.5 4.4 all-to-all-start.1
  49.8 3.8 copy.28
  53.6 19.8 %all-to-all-done.1 = bf16[128,8,896]{0,2,1:T(8,128)(2,1)S(1)} async-done(((bf16[128,8,896]{0,2,1:T(8,128)(2,1)}), bf16[128,8,896]{0,2,1:T(8,128)(2,1)S(1)}, u32[]{:S(2)}, u32[]{:S(2)}) %all-to-all-start.1) | async-done | bytes 1835040 | tf_op jit(solution)/shard_map/all_to_all | solution.py:47
  73.4 2.7 copy.30
  76.1 2.8 fusion.28
  78.9 2.4 convolution_add_fusion
  81.3 63.6 %all-reduce.6.cloned.1.call-done = f32[1024,448]{0,1:T(8,128)} async-done(((f32[1024,448]{0,1:T(8,128)}), f32[1024,448]{0,1:T(8,128)}) %all-reduce.6.cloned.1.call-update) | async-done | bytes 1835024 | tf_op jit(solution)/shard_map/psum | solution.py:52
  145.0 1.8 multiply_reduce_fusion.2
  146.8 33.4 %psum.71 = f32[1024]{0:T(1024)S(1)} all-reduce(f32[1024]{0:T(1024)S(1)} %multiply_reduce_fusion.2), channel_id=1, replica_groups=mesh['ctx'=8,'vocab'=16] {'vocab'}, use_global_device_ids=true, to_apply=%region_4.0 | all-reduce | flops 1024 | bytes 8192 | tf_op jit(solution)/shard_map/psum | solution.py:53
  181.4 1.1 multiply_convert_fusion.2
  182.7 103.4 %all-gather.2.cloned.1.call-done = bf16[1024,7168]{0,1:T(8,128)(2,1)} async-done(((bf16[1024,448]{0,1:T(8,128)(2,1)}), bf16[1024,7168]{0,1:T(8,128)(2,1)}) %all-gather.2.cloned.1.call-update) | async-done | bytes 14680080 | tf_op jit(solution)/shard_map/all_gather | solution.py:56
  286.2 14.3 %exponential_reduce_fusion = (f32[1024]{0:T(1024)S(1)}, f32[1024]{0:T(1024)S(1)}, f32[1024,512]{0,1:T(8,128)}) fusion(s32[512]{0:T(512)S(1)} %iota_add_fusion, s32[1024]{0:T(1024)S(1)} %copy-done.33, bf16[512,7168]{1,0:T(8,128)(2,1)} %param.17, bf16[1024,7168]{0,1:T(8,128)(2,1)} %all-gather.2.cloned.1.call-done), kind=kOutput, calls=%fused_computation.16 | convolution fusion | flops 7518287872 | bytes 24131584 | tf_op jit(solution)/shard_map/dot_general | solution.py:20
  300.4 64.9 %all-reduce = (f32[1024]{0:T(1024)S(1)}, f32[1024]{0:T(1024)S(1)}) all-reduce(f32[1024]{0:T(1024)S(1)} %get-tuple-element.16, f32[1024]{0:T(1024)S(1)} %get-tuple-element.15), channel_id=1, replica_groups=mesh['ctx'=8,'vocab'=16] {'ctx','vocab'}, use_global_device_ids=true, to_apply=%region_8.9 | all-reduce | flops 2048 | bytes 16384 | tf_op jit(solution)/shard_map/psum | solution.py:66
  365.9 14.2 %convolution_convert_fusion = bf16[1024,7168]{0,1:T(8,128)(2,1)} fusion(bf16[512,7168]{1,0:T(8,128)(2,1)} %param.17, f32[1024,512]{0,1:T(8,128)} %get-tuple-element.31, f32[1024]{0:T(1024)S(1)} %get-tuple-element.25, f32[1024]{0:T(1024)S(1)} %convert_element_type.64, s32[1024]{0:T(1024)S(1)} %copy-done.33, s32[512]{0:T(512)S(1)} %iota_add_fusion), kind=kOutput, calls=%fused_computation | convolution fusion | flops 7526678528 | bytes 24131584 | tf_op jit(solution)/shard_map/dot_general | solution.py:75
  380.2 99.1 %reduce-scatter.4.cloned.1.call-done = bf16[1024,448]{0,1:T(8,128)(2,1)} async-done(((bf16[1024,7168]{0,1:T(8,128)(2,1)}), bf16[1024,448]{0,1:T(8,128)(2,1)}) %reduce-scatter.4.cloned.1.call-update) | async-done | bytes 917520 | tf_op jit(solution)/shard_map/reduce_scatter | solution.py:76
  479.4 61.1 %all-reduce.8.cloned.1.call-done = bf16[1024,448]{0,1:T(8,128)(2,1)} async-done(((bf16[1024,448]{0,1:T(8,128)(2,1)}), bf16[1024,448]{0,1:T(8,128)(2,1)}) %all-reduce.8.cloned.1.call-update) | async-done | bytes 917520 | tf_op jit(solution)/shard_map/psum | solution.py:79
  540.5 2.5 fusion.10
  543.0 34.2 %psum.75 = f32[1024]{0:T(1024)} all-reduce(f32[1024]{0:T(1024)} %get-tuple-element.14), channel_id=1, replica_groups=mesh['ctx'=8,'vocab'=16] {'vocab'}, use_global_device_ids=true, to_apply=%region_13.14 | all-reduce | flops 1024 | bytes 8192 | tf_op jit(solution)/shard_map/psum | solution.py:82
  577.2 0.7 broadcast_multiply_fusion
  577.9 1.1 fusion.7
  579.1 1.3 convolution_convert_fusion.3
  580.4 35.8 %all_to_all.76 = bf16[8,128,896]{2,1,0:T(8,128)(2,1)S(1)} all-to-all(bf16[8,128,896]{2,1,0:T(8,128)(2,1)S(1)} %bitcast.39), channel_id=1, replica_groups=mesh['ctx'=8,'vocab'=16] {'ctx'}, dimensions={0} | all-to-all | bytes 3670016 | tf_op jit(solution)/shard_map/all_to_all | solution.py:92
  616.2 2.4 copy.31
  618.7 1.3 convolution_convert_fusion.2
  620.0 27.1 %all_to_all.77 = bf16[8,128,896]{2,1,0:T(8,128)(2,1)S(1)} all-to-all(bf16[8,128,896]{2,1,0:T(8,128)(2,1)S(1)} %bitcast.40), channel_id=1, replica_groups=mesh['ctx'=8,'vocab'=16] {'ctx'}, dimensions={0} | all-to-all | bytes 3670016 | tf_op jit(solution)/shard_map/all_to_all | solution.py:95
  647.1 2.4 copy.32
  649.6 3.7 convert_element_type.65
  653.3 1.3 dynamic_slice.12
  654.7 1.3 dynamic_slice.14
  656.0 2.1 convert_element_type.67
  658.8 14.1 %convolution_convert_fusion.1 = bf16[512,7168]{1,0:T(8,128)(2,1)} fusion(bf16[1024,7168]{0,1:T(8,128)(2,1)} %all-gather.2.cloned.1.call-done, f32[1024,512]{0,1:T(8,128)} %get-tuple-element.31, f32[1024]{0:T(1024)S(1)} %copy-done.26, f32[1024]{0:T(1024)S(1)} %copy-done.24, s32[1024]{0:T(1024)S(1)} %copy-done.34, s32[512]{0:T(512)S(1)} %copy-done.28), kind=kOutput, calls=%fused_computation.1 | convolution fusion | flops 7523008512 | bytes 24131584 | tf_op jit(solution)/shard_map/dot_general | solution.py:14
  672.9 2.0 convolution_convert_fusion.4
  675.0 2.0 convolution_convert_fusion.5
  677.0 9.2 %reduce-scatter.6.cloned.1.call-done = bf16[128,448]{0,1:T(8,128)(2,1)} async-done(((bf16[128,7168]{0,1:T(8,128)(2,1)}), bf16[128,448]{0,1:T(8,128)(2,1)}) %reduce-scatter.6.cloned.1.call-update) | async-done | bytes 114704 | tf_op jit(solution)/shard_map/reduce_scatter | solution.py:100
  686.2 1.2 fusion.22
  687.4 75.5 %reduce-scatter.8.cloned.1.call-done = bf16[128,448]{0,1:T(8,128)(2,1)} async-done(((bf16[128,7168]{0,1:T(8,128)(2,1)}), bf16[128,448]{0,1:T(8,128)(2,1)}) %reduce-scatter.8.cloned.1.call-update) | async-done | bytes 114704 | tf_op jit(solution)/shard_map/reduce_scatter | solution.py:103
  762.9 1.2 fusion.24
  764.2 30.9 %all-reduce.1 = (f32[128]{0:T(128)S(1)}, f32[128]{0:T(128)S(1)}) all-reduce(f32[128]{0:T(128)S(1)} %get-tuple-element.12, f32[128]{0:T(128)S(1)} %get-tuple-element.10), channel_id=1, replica_groups=mesh['ctx'=8,'vocab'=16] {'vocab'}, use_global_device_ids=true, to_apply=%region_16.17 | all-reduce | flops 256 | bytes 2048 | tf_op jit(solution)/shard_map/psum | solution.py:113
  795.1 21.9 %all-reduce.2 = (f32[448]{0:T(512)}, f32[448]{0:T(512)}) all-reduce(f32[448]{0:T(512)S(1)} %get-tuple-element.11, f32[448]{0:T(512)S(1)} %get-tuple-element.9), channel_id=1, replica_groups=mesh['ctx'=8,'vocab'=16] {'ctx'}, use_global_device_ids=true, to_apply=%region_21.22 | all-reduce | flops 896 | bytes 7168 | tf_op jit(solution)/shard_map/psum | solution.py:132
  817.0 2.1 fusion.16
  (90 shorter events, 3.9 us)
Async XLA Ops:
  7.2 68.9 %copy-start = (bf16[896,448]{0,1:T(8,128)(2,1)S(1)}, bf16[896,448]{0,1:T(8,128)(2,1)}, u32[]{:S(2)}) copy-start(bf16[896,448]{0,1:T(8,128)(2,1)} %param.14) | copy-start | bytes 2408452
  7.2 5.0 copy-start.13
  10.6 5.5 copy-start.5
  12.1 3.9 copy-start.19
  16.0 29.4 %all-to-all-start = ((bf16[128,8,896]{0,2,1:T(8,128)(2,1)}), bf16[128,8,896]{0,2,1:T(8,128)(2,1)}, u32[]{:S(2)}, u32[]{:S(2)}) async-start(bf16[128,8,896]{0,2,1:T(8,128)(2,1)} %bitcast.32), calls=%async_computation | async-start | bytes 3670016 | tf_op jit(solution)/shard_map/all_to_all | solution.py:46
  21.8 5.3 copy-start.14
  25.1 5.9 copy-start.3
  26.7 0.5 copy-start.21
  45.5 27.9 %all-to-all-start.1 = ((bf16[128,8,896]{0,2,1:T(8,128)(2,1)}), bf16[128,8,896]{0,2,1:T(8,128)(2,1)S(1)}, u32[]{:S(2)}, u32[]{:S(2)}) async-start(bf16[128,8,896]{0,2,1:T(8,128)(2,1)} %bitcast.30), calls=%async_computation.1 | async-start | bytes 3670016 | tf_op jit(solution)/shard_map/all_to_all | solution.py:47
  49.8 95.1 %all-reduce.6.cloned.1.call-start = ((), (), s32[]{:S(2)}) async-start(), calls=%async_computation.7 | async-start | bytes 3670016 | tf_op jit(solution)/shard_map/psum | solution.py:52
  76.1 2.8 copy-start.8
  76.1 2.8 copy-start.31
  81.3 100.2 %copy-start.17 = (f32[448]{0:T(512)S(1)}, f32[448]{0:T(512)}, u32[]{:S(2)}) copy-start(f32[448]{0:T(512)} %param.16) | copy-start | bytes 5380
  81.3 204.9 %all-gather.2.cloned.1.call-start = ((), (), s32[]{:S(2)}) async-start(), calls=%async_computation.8 | async-start | bytes 15597568 | tf_op jit(solution)/shard_map/all_gather | solution.py:56
  145.0 36.5 %copy-start.2 = (f32[1024,448]{0,1:T(8,128)S(1)}, f32[1024,448]{0,1:T(8,128)}, u32[]{:S(2)}) copy-start(f32[1024,448]{0,1:T(8,128)} %all-reduce.6.cloned.1.call-done) | copy-start | bytes 5505028
  146.8 35.9 %copy-start.18 = (s32[1024]{0:T(1024)S(1)}, s32[1024]{0:T(1024)}, u32[]{:S(2)}) copy-start(s32[1024]{0:T(1024)} %param.19) | copy-start | bytes 12292
  146.8 139.4 %copy-start.33 = (s32[1024]{0:T(1024)S(1)}, s32[1024]{0:T(1024)}, u32[]{:S(2)}) copy-start(s32[1024]{0:T(1024)} %param.18) | copy-start | bytes 12292
  180.8 0.6 copy-start.12
  182.6 296.7 %reduce-scatter.4.cloned.1.call-start = ((), (), s32[]{:S(2)}) async-start(), calls=%async_computation.9 | async-start | bytes 15597568 | tf_op jit(solution)/shard_map/reduce_scatter | solution.py:76
  182.7 183.3 %copy-start.23 = (f32[1024]{0:T(1024)}, f32[1024]{0:T(1024)S(1)}, u32[]{:S(2)}) copy-start(f32[1024]{0:T(1024)S(1)} %convert_element_type.64) | copy-start | bytes 12292
  182.7 183.2 %copy-start.27 = (s32[512]{0:T(512)}, s32[512]{0:T(512)S(1)}, u32[]{:S(2)}) copy-start(s32[512]{0:T(512)S(1)} %iota_add_fusion) | copy-start | bytes 6148
  365.9 14.2 %copy-start.25 = (f32[1024]{0:T(1024)}, f32[1024]{0:T(1024)S(1)}, u32[]{:S(2)}) copy-start(f32[1024]{0:T(1024)S(1)} %get-tuple-element.25) | copy-start | bytes 12292
  380.1 160.4 %all-reduce.8.cloned.1.call-start = ((), (), s32[]{:S(2)}) async-start(), calls=%async_computation.10 | async-start | bytes 1835008 | tf_op jit(solution)/shard_map/psum | solution.py:79
  479.4 206.8 %reduce-scatter.6.cloned.1.call-start = ((), (), s32[]{:S(2)}) async-start(), calls=%async_computation.11 | async-start | bytes 1949696 | tf_op jit(solution)/shard_map/reduce_scatter | solution.py:100
  540.5 37.4 %copy-start.6 = (bf16[1024,448]{0,1:T(8,128)(2,1)S(1)}, bf16[1024,448]{0,1:T(8,128)(2,1)}, u32[]{:S(2)}) copy-start(bf16[1024,448]{0,1:T(8,128)(2,1)} %all-reduce.8.cloned.1.call-done) | copy-start | bytes 2752516
  579.1 1.3 copy-start.10
  616.2 2.5 copy-start.11
  616.2 2.5 copy-start.32
  618.7 144.3 %reduce-scatter.8.cloned.1.call-start = ((), (), s32[]{:S(2)}) async-start(), calls=%async_computation.12 | async-start | bytes 1949696 | tf_op jit(solution)/shard_map/reduce_scatter | solution.py:103
  649.6 6.4 copy-start.4
  656.0 2.7 copy-start.24
  656.0 2.7 copy-start.26
  656.0 2.8 copy-start.28
  656.0 2.8 copy-start.34
  658.8 14.1 %copy-start.9 = (bf16[8,128,896]{2,1,0:T(8,128)(2,1)S(1)}, bf16[8,128,896]{2,1,0:T(8,128)(2,1)}, u32[]{:S(2)}) copy-start(bf16[8,128,896]{2,1,0:T(8,128)(2,1)} %copy.30) | copy-start | bytes 5505028
  672.9 2.0 copy-start.7
  674.9 11.3 %copy-start.15 = (f32[448]{0:T(512)S(1)}, f32[448]{0:T(512)}, u32[]{:S(2)}) copy-start(f32[448]{0:T(512)} %dynamic_slice.12) | copy-start | bytes 5380
  674.9 11.3 %copy-start.20 = (f32[128]{0:T(128)S(1)}, f32[128]{0:T(128)}, u32[]{:S(2)}) copy-start(f32[128]{0:T(128)} %copy-done.19) | copy-start | bytes 1540
  674.9 88.0 %copy-start.16 = (f32[448]{0:T(512)S(1)}, f32[448]{0:T(512)}, u32[]{:S(2)}) copy-start(f32[448]{0:T(512)} %dynamic_slice.14) | copy-start | bytes 5380
  674.9 88.0 %copy-start.22 = (f32[128]{0:T(128)S(1)}, f32[128]{0:T(128)}, u32[]{:S(2)}) copy-start(f32[128]{0:T(128)} %copy-done.21) | copy-start | bytes 1540
  674.9 142.0 %copy-start.29 = (f32[128]{0:T(128)S(1)}, f32[128]{0:T(128)}, u32[]{:S(2)}) copy-start(f32[128]{0:T(128)} %get-tuple-element.29) | copy-start | bytes 1540
  674.9 142.0 %copy-start.30 = (f32[128]{0:T(128)S(1)}, f32[128]{0:T(128)}, u32[]{:S(2)}) copy-start(f32[128]{0:T(128)} %get-tuple-element.27) | copy-start | bytes 1540
  674.9 144.1 %copy-start.1 = (bf16[896,448]{0,1:T(8,128)(2,1)S(1)}, bf16[896,448]{0,1:T(8,128)(2,1)}, u32[]{:S(2)}) copy-start(bf16[896,448]{0,1:T(8,128)(2,1)} %param.14) | copy-start | bytes 2408452
Sparse Core Ops, SparseCore 0:
  81.4 63.5 all-reduce.5
  182.7 103.3 all-gather.1
  380.3 99.0 reduce-scatter.3
  481.5 58.9 all-reduce.7
  618.8 67.3 reduce-scatter.5
  689.6 73.2 reduce-scatter.7
where the time goes:
time: 828 us; the launch traced here: 827 us
  waiting for transfers between devices  446 us (54%)
  blocking collectives  248 us (30%)
  matrix products  54.3 us (7%)
  other arithmetic  29.6 us (4%)
  local copies, waits for them, and re-layouts  21.9 us (3%)
  between operations  16.2 us (2%)
  starting transfers between devices  10.4 us (1%)
    all_gather x1, waiting for transfers between devices, local(): normed_rows = lax.all_gather(normed_piece, 'vocab', axis=1, tiled=True)  103 us
    reduce_scatter x1, waiting for transfers between devices, local(): lax.psum_scatter(normed_part.astype(jnp.bfloat16), 'vocab', scatter_dimen...  99.1 us
    reduce_scatter x1, waiting for transfers between devices, local(): lax.psum_scatter(embed_tokens.astype(jnp.bfloat16), 'vocab', scatter_dime...  75.5 us
    psum x1, blocking collectives, local(): lax.psum((exp_part, target_part), ('ctx', 'vocab'))  64.9 us
    psum x1, waiting for transfers between devices, local(): projected = lax.psum(partial_proj, 'ctx')  63.6 us
    psum x1, waiting for transfers between devices, local(): normed_grad = lax.psum(vocab_summed, 'ctx').astype(jnp.float32)  61.1 us
    all_to_all x1, blocking collectives, local(): lax.all_to_all(hidden_part.astype(jnp.bfloat16), 'ctx', split_axis=0, con...  35.8 us
    psum x1, blocking collectives, local(): row_dot = lax.psum(jnp.sum(scaled_grad * projected, axis=-1), 'vocab')  34.2 us
  transfers between devices with their start and end apart: 8, of which 8 were waited for; matrix products, arithmetic and copies ran while one was open for 5% of the time, Pallas kernels for 0%

commit v1 on v0

v1 whole, which is shorter than its diff:
```python
import functools

import jax
import jax.numpy as jnp
from jax import lax
from jax.experimental import pallas as pl
from jax.experimental.pallas import tpu as pltpu
from jax.sharding import PartitionSpec as P

EPSILON = 1e-06
MESH = pl.DeviceIdType.MESH
VMEM = pl.BlockSpec(memory_space=pltpu.VMEM)
ANY = pl.BlockSpec(memory_space=pl.ANY)
F32 = jnp.float32
BF16 = jnp.bfloat16
PARTS = ((0, 640, "xyz"), (640, 640, "yzx"), (1280, 512, "zxy"))


class Place:
    def __init__(self):
        self.ctx = lax.axis_index("ctx")
        self.v = lax.axis_index("vocab")
        self.c = {"x": self.ctx // 2, "y": self.v // 4, "z": self.v % 4}
        self.core = self.ctx % 2

    def at(self, ctx=None, v=None):
        return {"ctx": self.ctx if ctx is None else ctx, "vocab": self.v if v is None else v}

    def along(self, axis, step):
        i = lax.rem(self.c[axis] + step + 4, 4)
        if axis == "x":
            return self.at(ctx=i * 2 + self.core)
        if axis == "y":
            return self.at(v=i * 4 + self.c["z"])
        return self.at(v=self.c["y"] * 4 + i)

    def sibling(self):
        return self.at(ctx=self.c["x"] * 2 + 1 - self.core)

    def ctx_peer(self, o):
        return self.at(ctx=lax.rem(self.ctx + o, 8))

    def v_peer(self, o):
        return self.at(v=lax.rem(self.v + o, 16))


class Copies:
    def __init__(self, send, recv):
        self.send, self.recv, self.count, self.started = send, recv, 0, []

    def go(self, src, dst, device):
        copy = pltpu.make_async_remote_copy(
            src_ref=src,
            dst_ref=dst,
            send_sem=self.send.at[self.count],
            recv_sem=self.recv.at[self.count],
            device_id=device,
            device_id_type=MESH,
        )
        self.count += 1
        copy.start()
        self.started.append(copy)
        return copy

    def finish(self):
        for copy in self.started:
            copy.wait_send()
        self.started = []


def greet(devices):
    barrier = pltpu.get_barrier_semaphore()
    for device in devices:
        pl.semaphore_signal(barrier, inc=1, device_id=device, device_id_type=MESH)
    pl.semaphore_wait(barrier, len(devices))


def run(*rings):
    rings = list(rings)
    while rings:
        left = []
        for ring in rings:
            try:
                next(ring)
                left.append(ring)
            except StopIteration:
                pass
        rings = left


def chain(*makers):
    for maker in makers:
        yield from maker()


def gather_ring(copies, here, axis, slab):
    me = here.c[axis]
    right, left = here.along(axis, 1), here.along(axis, -1)
    before, after = lax.rem(me + 3, 4), lax.rem(me + 1, 4)
    from_left = copies.go(slab(me, None), slab(me, None), right)
    from_right = copies.go(slab(me, None), slab(me, None), left)
    yield
    from_left.wait_recv()
    far_a = copies.go(slab(before, 0), slab(before, 0), right)
    from_right.wait_recv()
    far_b = copies.go(slab(after, 1), slab(after, 1), left)
    yield
    far_a.wait_recv()
    far_b.wait_recv()


def reduce_ring(copies, here, axis, slab, half, one, two, held, add):
    me = here.c[axis]
    right, left = here.along(axis, 1), here.along(axis, -1)
    before, after, far = lax.rem(me + 3, 4), lax.rem(me + 1, 4), lax.rem(me + 2, 4)
    a1 = copies.go(slab(far, 0), one.at[0], right)
    b1 = copies.go(slab(far, 1), one.at[1], left)
    a2 = copies.go(slab(after, 1), half(two.at[0], 1), right)
    b2 = copies.go(slab(before, 0), half(two.at[1], 0), left)
    yield
    a1.wait_recv()
    add(held.at[0], (slab(after, 0), one.at[0]))
    a3 = copies.go(held.at[0], half(two.at[0], 0), right)
    b1.wait_recv()
    add(held.at[1], (slab(before, 1), one.at[1]))
    b3 = copies.go(held.at[1], half(two.at[1], 1), left)
    yield
    a2.wait_recv()
    b2.wait_recv()
    a3.wait_recv()
    b3.wait_recv()


def add_refs(out, terms):
    lead = out.shape[:-2]
    total = 1
    for n in lead:
        total *= n

    def block(index):
        acc = terms[0][index].astype(F32)
        for term in terms[1:]:
            acc = acc + term[index].astype(F32)
        out[index] = acc.astype(out.dtype)

    if total == 1:
        block(tuple(0 for _ in lead) + (slice(None), slice(None)))
        return

    @pl.loop(0, total)
    def _(i):
        index = []
        for n in reversed(lead):
            index.append(i % n)
            i = i // n
        block(tuple(reversed(index)) + (slice(None), slice(None)))


def columns_kernel(rows, head, cols, head_sib, send, recv, local_sem):
    here = Place()
    copies = Copies(send, recv)
    greet(
        [here.ctx_peer(o) for o in range(1, 8)]
        + [here.along("y", 1), here.along("y", -1), here.along("z", 1), here.along("z", -1)]
    )
    y, z = here.c["y"], here.c["z"]

    def block(c):
        return cols.at[y // 2, c, y % 2, z]

    arrivals = []
    for o in range(1, 8):
        peer = lax.rem(here.ctx + o, 8)
        arrivals.append(copies.go(rows.at[peer], block(here.ctx), here.ctx_peer(o)))
    own = pltpu.make_async_copy(rows.at[here.ctx], block(here.ctx), local_sem)
    own.start()
    swap = copies.go(head, head_sib, here.sibling())
    own.wait()
    for arrival in arrivals:
        arrival.wait_recv()

    def span(h):
        return slice(None) if h is None else pl.ds(h * 4, 4)

    def y_first(i, h):
        return cols.at[i // 2, span(h), i % 2, z]

    def z_last(i, h):
        return cols.at[:, span(h), :, i]

    def z_first(i, h):
        return cols.at[y // 2, span(h), y % 2, i]

    def y_last(i, h):
        return cols.at[i // 2, span(h), i % 2]

    def both(first, second):
        run(
            chain(
                lambda: gather_ring(copies, here, *first), lambda: gather_ring(copies, here, *second)
            )
        )

    mark, kept = copies.count, copies.started
    copies.started = []

    @pl.when(here.core == 0)
    def _():
        both(("y", y_first), ("z", z_last))
        copies.finish()

    copies.count = mark

    @pl.when(here.core == 1)
    def _():
        both(("z", z_first), ("y", y_last))
        copies.finish()

    copies.started = kept
    swap.wait_recv()
    copies.finish()


def rows_kernel(
    partial, gain, projected, scales, rows,
    sib, summed, one, two, held, squares, mine_sq, piece, pieces, block, send, recv, local_sem,
):
    here = Place()
    copies = Copies(send, recv)
    rings = [here.along(a, s) for a in "xyz" for s in (1, -1)]
    greet(
        rings
        + [here.sibling()]
        + [here.v_peer(o) for o in range(1, 16)]
        + [here.along(a, 2) for a in "x"]
    )
    width = 7168
    x, y, z = here.c["x"], here.c["y"], here.c["z"]
    swap = copies.go(partial.at[:, 1 - here.core], sib, here.sibling())
    swap.wait_recv()
    for i in range(4):
        summed[i] = partial[i, here.core] + sib[i]

    def half(ref, h):
        return ref.at[pl.ds(h * 64, 64)]

    run(
        reduce_ring(
            copies, here, "x",
            lambda i, h: half(summed.at[i], h), half, one, two, held,
            lambda out, terms: out.__setitem__(..., terms[0][...] + terms[1][...]),
        )
    )
    total = summed[x] + two[0] + two[1]
    projected[...] = total
    mine_sq[...] = lax.dot_general(
        jnp.ones((8, total.shape[1]), F32), total * total, (((1,), (1,)), ((), ())),
        precision=lax.Precision.HIGHEST, preferred_element_type=F32,
    )
    piece[...] = (total * gain[...]).astype(BF16).reshape(piece.shape)
    exchange = []
    for o in range(1, 4):
        to = lax.rem(z + o, 4)
        exchange.append(copies.go(piece.at[to], pieces.at[z], here.along("z", o)))
    sq_in = []
    for o in range(1, 16):
        sq_in.append(copies.go(mine_sq, squares.at[here.v], here.v_peer(o)))
    squares[here.v] = mine_sq[...]
    pieces[z] = piece[z]
    for copy in exchange:
        copy.wait_recv()
    for i in range(4):
        block[:, i * 448 : (i + 1) * 448] = pieces[i]
    own = pltpu.make_async_copy(block, rows.at[y, x, z], local_sem)
    own.start()
    own.wait()

    def stage(part, k):
        off, w, order = part

        def slab(i, h):
            index = []
            for a in "yxz":
                at = order.index(a)
                index.append(i if at == k else slice(None) if at < k else here.c[a])
            lines = slice(None) if h is None else pl.ds(h * 16, 16)
            return rows.at[(*index, lines, pl.ds(off, w))]

        return lambda: gather_ring(copies, here, order[k], slab)

    def scale():
        yield
        for copy in sq_in:
            copy.wait_recv()
        scales[x] = lax.rsqrt(jnp.sum(squares[...], axis=0) / width + EPSILON)
        out = [copies.go(scales.at[x], scales.at[x], here.along("x", o)) for o in range(1, 4)]
        yield
        yield
        for copy in out:
            copy.wait_recv()

    run(*[chain(*[stage(part, k) for k in range(3)]) for part in PARTS], scale())
    copies.finish()


def totals_kernel(tile, out, group, line, part, send, recv):
    here = Place()
    copies = Copies(send, recv)
    greet(
        [here.v_peer(o) for o in range(1, 16)]
        + [here.along("x", o) for o in (1, 2, 3)]
        + [here.sibling()]
    )
    group[here.v] = tile[...]
    ins = [copies.go(tile, group.at[here.v], here.v_peer(o)) for o in range(1, 16)]
    for copy in ins:
        copy.wait_recv()
    x = here.c["x"]
    line[x] = jnp.sum(group[...], axis=0)
    ins = [copies.go(line.at[x], line.at[x], here.along("x", o)) for o in (1, 2, 3)]
    for copy in ins:
        copy.wait_recv()
    out[here.core] = jnp.sum(line[...], axis=0)
    copies.go(out.at[here.core], out.at[here.core], here.sibling()).wait_recv()
    copies.finish()


def drop(shape, axes, axis):
    return tuple(n for n, a in zip(shape, axes) if a != axis)


def grad_kernel(
    terms, projected, gain, scale, rows, lgr,
    proj_grad, gain_grad, rows_sib, lgr_sib, *scratch,
):
    rings_scratch, (whole, piece, pieces, dots, mine_dot, gains, mine_gain, send, recv) = (
        scratch[:-9],
        scratch[-9:],
    )
    here = Place()
    copies = Copies(send, recv)
    greet(
        [here.along(a, s) for a in "xyz" for s in (1, -1)]
        + [here.along("z", 2)]
        + [here.v_peer(o) for o in range(1, 16)]
        + [here.ctx_peer(o) for o in range(1, 8)]
    )
    width = 7168
    z = here.c["z"]
    swaps = [
        copies.go(lgr.at[1], lgr_sib, here.sibling()),
        copies.go(rows, rows_sib, here.sibling()),
    ]

    def half(ref, h):
        index = (slice(None),) * (len(ref.shape) - 2) + (pl.ds(h * 16, 16),)
        return ref.at[index]

    def part_rings(n, part):
        off, w, order = part
        order = order[::-1]
        axes = "yxz"
        source = terms
        cols = pl.ds(off, w)
        for k in range(3):
            one, two, held, out = rings_scratch[(n * 3 + k) * 4 : (n * 3 + k) * 4 + 4]
            axis = order[k]

            def slab(i, h, source=source, axes=axes, cols=cols, axis=axis):
                index = tuple(i if a == axis else slice(None) for a in axes)
                lines = slice(None) if h is None else pl.ds(h * 16, 16)
                return source.at[(*index, lines, cols)]

            yield from reduce_ring(
                copies, here, axis, slab, half, one, two, held, add_refs
            )
            if k < 2:
                add_refs(out, (slab(here.c[axis], None), two.at[0], two.at[1]))
            else:
                own = slab(here.c[axis], None)[...].astype(F32)
                whole[:, off : off + w] = own + two[0].astype(F32) + two[1].astype(F32)
            source, cols = out, slice(None)
            axes = axes.replace(axis, "")
            yield

    run(*[part_rings(n, part) for n, part in enumerate(PARTS)])
    for i in range(4):
        piece[i] = whole[:, i * 448 : (i + 1) * 448]
    exchange = []
    for o in range(1, 4):
        to = lax.rem(z + o, 4)
        exchange.append(copies.go(piece.at[to], pieces.at[z], here.along("z", o)))
    pieces[z] = piece[z]
    for copy in exchange:
        copy.wait_recv()
    normed_grad = pieces[...].reshape(128, 448)
    wide = projected[...]
    row_scale = scale[...]
    scaled = normed_grad * gain[...]
    mine_dot[...] = lax.dot_general(
        jnp.ones((8, 448), F32), scaled * wide, (((1,), (1,)), ((), ())),
        precision=lax.Precision.HIGHEST, preferred_element_type=F32,
    )
    ins = [copies.go(mine_dot, dots.at[here.v], here.v_peer(o)) for o in range(1, 16)]
    dots[here.v] = mine_dot[...]
    mine_gain[...] = jnp.broadcast_to(
        jnp.sum(normed_grad * wide * row_scale, axis=0, keepdims=True), (8, 448)
    )
    gain_ins = [copies.go(mine_gain, gains.at[here.ctx], here.ctx_peer(o)) for o in range(1, 8)]
    gains[here.ctx] = mine_gain[...]
    for copy in ins:
        copy.wait_recv()
    row_dot = jnp.sum(dots[...], axis=0).T[:, :1]
    grad = row_scale * scaled - wide * (row_scale * row_scale * row_scale) * (row_dot / width)
    x, core = here.c["x"], here.core
    proj_grad[x, core] = grad.astype(BF16)

    def slab(i, h):
        lines = slice(None) if h is None else pl.ds(h * 64, 64)
        return proj_grad.at[i, core, lines]

    run(gather_ring(copies, here, "x", slab))
    copies.go(proj_grad.at[:, core], proj_grad.at[:, core], here.sibling()).wait_recv()
    for copy in gain_ins:
        copy.wait_recv()
    gain_grad[...] = jnp.sum(gains[...], axis=0)[:1]
    for copy in swaps:
        copy.wait_recv()
    copies.finish()


def back_kernel(
    terms, inputs, gains, scales, grads, gain_grads,
    one_a, two_a, held_a, out_a, one_b, two_b, held_b, out_b,
    one_c, two_c, held_c, one_d, two_d, held_d,
    summed, sent, got, mine_dot, dots, mine_gain, gain_all, send, recv, send_far, recv_far,
):
    here = Place()
    copies = Copies(send, recv)
    y, z, v, ctx = here.c["y"], here.c["z"], here.v, here.ctx
    width = 7168
    barrier = pltpu.get_barrier_semaphore()
    near = (
        [here.along(a, s) for a in "yz" for s in (1, -1)]
        + [here.v_peer(o) for o in range(1, 16)]
        + [here.ctx_peer(o) for o in range(1, 8)]
    )
    for device in near:
        pl.semaphore_signal(barrier, inc=1, device_id=device, device_id_type=MESH)
    for source in range(16):
        pl.semaphore_signal(
            barrier, inc=1, device_id=here.at(ctx=v // 2, v=source), device_id_type=MESH
        )
    pl.semaphore_wait(barrier, len(near) + 16)

    def span(h):
        return slice(None) if h is None else pl.ds(h * 4, 4)

    def back_y(i, h):
        return terms.at[i // 2, span(h), i % 2]

    def back_z(i, h):
        return terms.at[:, span(h), :, i]

    @pl.when(here.core == 0)
    def _():
        run(
            reduce_ring(
                copies, here, "y", back_y, lambda ref, h: ref.at[span(h)],
                one_a, two_a, held_a, add_refs,
            )
        )
        add_refs(out_a, (back_y(y, None), two_a.at[0], two_a.at[1]))
        run(
            reduce_ring(
                copies, here, "z", lambda i, h: out_a.at[span(h), i],
                lambda ref, h: ref.at[span(h)], one_c, two_c, held_c, add_refs,
            )
        )
        add_refs(summed, (out_a.at[:, z], two_c.at[0], two_c.at[1]))
        copies.finish()

    copies.count = 0

    @pl.when(here.core == 1)
    def _():
        run(
            reduce_ring(
                copies, here, "z", back_z, lambda ref, h: ref.at[:, span(h)],
                one_b, two_b, held_b, add_refs,
            )
        )
        add_refs(out_b, (back_z(z, None), two_b.at[0], two_b.at[1]))
        run(
            reduce_ring(
                copies, here, "y", lambda i, h: out_b.at[i // 2, span(h), i % 2],
                lambda ref, h: ref.at[span(h)], one_d, two_d, held_d, add_refs,
            )
        )
        add_refs(summed, (out_b.at[y // 2, :, y % 2], two_d.at[0], two_d.at[1]))
        copies.finish()

    @pl.loop(0, 8)
    def _(c):
        sent[0, c] = summed[c][:, :448].astype(BF16)
        sent[1, c] = summed[c][:, 448:].astype(BF16)

    def far_copy(o, s):
        to = lax.rem(ctx + o, 8)
        return pltpu.make_async_remote_copy(
            src_ref=sent.at[s, to],
            dst_ref=got.at[v // 8, pl.ds(lax.rem(v, 8) * 16, 16)],
            send_sem=send_far.at[o * 2 + s],
            recv_sem=recv_far.at[v],
            device_id=here.at(ctx=to, v=ctx * 2 + s),
            device_id_type=MESH,
        )

    for o in range(8):
        for s in range(2):
            if o:
                far_copy(o, s).start()
            else:

                @pl.when(v != ctx * 2 + s)
                def _(s=s):
                    far_copy(0, s).start()

                @pl.when(v == ctx * 2 + s)
                def _(s=s):
                    got[v // 8, pl.ds(lax.rem(v, 8) * 16, 16)] = sent[s, ctx]

    for source in range(16):

        @pl.when(jnp.logical_or(ctx != v // 2, v != source))
        def _(source=source):
            pltpu.make_async_remote_copy(
                src_ref=sent.at[0, 0],
                dst_ref=got.at[source // 8, pl.ds(source % 8 * 16, 16)],
                send_sem=send_far.at[0],
                recv_sem=recv_far.at[source],
                device_id=here.at(ctx=lax.rem(ctx + 1, 8)),
                device_id_type=MESH,
            ).wait_recv()

    for e in range(2):
        back = got[e].astype(F32)
        wide = inputs[e].astype(F32)
        mine_dot[e] = lax.dot_general(
            jnp.ones((8, 448), F32), back * gains[e] * wide, (((1,), (1,)), ((), ())),
            precision=lax.Precision.HIGHEST, preferred_element_type=F32,
        )
        mine_gain[e] = jnp.broadcast_to(
            jnp.sum(back * wide * scales[e], axis=0, keepdims=True), (8, 448)
        )
    ins = [copies.go(mine_dot, dots.at[v], here.v_peer(o)) for o in range(1, 16)]
    gain_ins = [copies.go(mine_gain, gain_all.at[ctx], here.ctx_peer(o)) for o in range(1, 8)]
    dots[v] = mine_dot[...]
    gain_all[ctx] = mine_gain[...]
    for copy in ins:
        copy.wait_recv()
    for e in range(2):
        back = got[e].astype(F32)
        wide = inputs[e].astype(F32)
        dot = jnp.sum(dots[:, e], axis=0).T[:, :1]
        scale = scales[e]
        grads[e] = (
            scale * (back * gains[e]) - wide * (scale * scale * scale) * (dot / width)
        ).astype(BF16)
    for copy in gain_ins:
        copy.wait_recv()
    gain_grads[...] = jnp.sum(gain_all[...], axis=0)
    for o in range(8):
        for s in range(2):
            if o:
                far_copy(o, s).wait_send()
            else:

                @pl.when(v != ctx * 2 + s)
                def _(s=s):
                    far_copy(0, s).wait_send()

    copies.finish()


def logits_kernel(rows, own, sib, out):
    @pl.when(pl.program_id(0) == 0)
    def _():
        out[...] = jnp.zeros_like(out)

    for h, head in enumerate((own, sib)):
        out[:, h * 512 : (h + 1) * 512] += lax.dot_general(
            rows[0], head[...], (((1,), (1,)), ((), ())), preferred_element_type=F32
        )


def normed_kernel(grad, own, sib, out):
    out[0] = (
        jnp.dot(grad[:, :512], own[...], preferred_element_type=F32)
        + jnp.dot(grad[:, 512:], sib[...], preferred_element_type=F32)
    ).astype(BF16)


def head_kernel(own_grad, sib_grad, own, sib, out):
    out[...] = (
        jnp.dot(own_grad[...], own[0], preferred_element_type=F32)
        + jnp.dot(sib_grad[...], sib[0], preferred_element_type=F32)
    ).astype(BF16)


def params(number, limit=56):
    return pltpu.CompilerParams(
        collective_id=number, has_side_effects=True, vmem_limit_bytes=limit * 2**20
    )


def plain():
    return pltpu.CompilerParams(vmem_limit_bytes=56 * 2**20)


def sems(n):
    return [pltpu.SemaphoreType.DMA((n,)), pltpu.SemaphoreType.DMA((n,))]


def shape(dims, kind):
    return jax.ShapeDtypeStruct(dims, kind)


def reduce_scratch():
    scratch = []
    for _, w, order in PARTS:
        dims = (4, 4)
        for k in range(3):
            scratch += [
                pltpu.VMEM((2, *dims, 16, w), BF16),
                pltpu.VMEM((2, *dims, 32, w), BF16),
                pltpu.VMEM((2, *dims, 16, w), BF16),
                pltpu.VMEM((*dims, 32, w), BF16),
            ]
            dims = dims[1:]
    return scratch


def scale_of(values):
    return lax.rsqrt(jnp.mean(values * values, axis=-1, keepdims=True) + EPSILON)


def contract_first(left, right):
    return lax.dot_general(
        left, right, (((0,), (0,)), ((), ())), preferred_element_type=F32
    )


def contract_last(left, right):
    return lax.dot_general(
        left, right, (((1,), (1,)), ((), ())), preferred_element_type=F32
    )


def local(
    hidden_state, embedded_next, gain_hidden, gain_embed, proj_hidden, proj_embed,
    final_gain, head, targets, loss_mask,
):
    width = hidden_state.shape[1]
    token_total = targets.shape[0]
    ctx, v = lax.axis_index("ctx"), lax.axis_index("vocab")
    x, core = ctx // 2, ctx % 2
    sliver = (v % 8) * 16
    first = v < 8
    raw = jnp.where(
        first,
        lax.dynamic_slice_in_dim(hidden_state, sliver, 16, 0),
        lax.dynamic_slice_in_dim(embedded_next, sliver, 16, 0),
    ).astype(F32)
    gain_in = jnp.where(first, gain_hidden, gain_embed)
    normed = (raw * scale_of(raw) * gain_in).astype(BF16)
    normed = normed.reshape(16, 8, 896).transpose(1, 0, 2)

    cols, head_sib = pl.pallas_call(
        columns_kernel,
        out_shape=[shape((2, 8, 2, 4, 16, 896), BF16), shape(head.shape, BF16)],
        in_specs=[VMEM, ANY],
        out_specs=[ANY, ANY],
        scratch_shapes=sems(16) + [pltpu.SemaphoreType.DMA],
        compiler_params=params(1),
        name="columns",
    )(normed, head)
    hidden_cols = cols[0].reshape(1024, 896)
    embed_cols = cols[1].reshape(1024, 896)
    partial = jnp.dot(hidden_cols, proj_hidden, preferred_element_type=F32) + jnp.dot(
        embed_cols, proj_embed, preferred_element_type=F32
    )

    projected, scales, rows = pl.pallas_call(
        rows_kernel,
        out_shape=[
            shape((128, 448), F32), shape((4, 8, 128), F32), shape((4, 4, 4, 32, 1792), BF16),
        ],
        in_specs=[VMEM, VMEM],
        out_specs=[VMEM, VMEM, ANY],
        scratch_shapes=[
            pltpu.VMEM((4, 128, 448), F32),
            pltpu.VMEM((4, 128, 448), F32),
            pltpu.VMEM((2, 64, 448), F32),
            pltpu.VMEM((2, 128, 448), F32),
            pltpu.VMEM((2, 64, 448), F32),
            pltpu.VMEM((16, 8, 128), F32),
            pltpu.VMEM((8, 128), F32),
            pltpu.VMEM((4, 32, 448), BF16),
            pltpu.VMEM((4, 32, 448), BF16),
            pltpu.VMEM((32, 1792), BF16),
        ]
        + sems(72)
        + [pltpu.SemaphoreType.DMA],
        compiler_params=params(2),
        name="rows",
    )(partial.reshape(4, 2, 128, 448), final_gain[None, :])

    gathered = rows.reshape(4, 512, 1792)
    row_scale = scales[:, 0].reshape(512, 1)
    block = pl.BlockSpec((1, 512, 1792), lambda i: (i, 0, 0))
    head_block = pl.BlockSpec((512, 1792), lambda i: (0, i))
    fixed = pl.BlockSpec((512, 1024), lambda i: (0, 0))
    raw_logits = pl.pallas_call(
        logits_kernel,
        grid=(4,),
        out_shape=shape((512, 1024), F32),
        in_specs=[block, head_block, head_block],
        out_specs=fixed,
        compiler_params=plain(),
        name="logits",
    )(gathered, head, head_sib)
    logits = raw_logits * row_scale
    own_ids = (ctx * 16 + v) * 512 + lax.iota(jnp.int32, 512)
    sib_ids = ((ctx + 1 - 2 * core) * 16 + v) * 512 + lax.iota(jnp.int32, 512)
    vocab_ids = jnp.concatenate([own_ids, sib_ids])

    def of_core(values, k):
        return lax.dynamic_index_in_dim(values.reshape(4, 2, 128), k, 1, keepdims=False)

    my_targets = of_core(targets, core).reshape(512)
    mask = of_core(loss_mask, core).reshape(512).astype(F32)
    is_target = my_targets[:, None] == vocab_ids[None, :]
    exp_part = jnp.sum(jnp.exp(logits), axis=-1)
    target_part = jnp.sum(jnp.where(is_target, logits, F32(0.0)), axis=-1)
    tile = jnp.concatenate([exp_part.reshape(4, 128), target_part.reshape(4, 128)])

    totals = pl.pallas_call(
        totals_kernel,
        out_shape=shape((2, 8, 128), F32),
        in_specs=[VMEM],
        out_specs=VMEM,
        scratch_shapes=[
            pltpu.VMEM((16, 8, 128), F32), pltpu.VMEM((4, 8, 128), F32), pltpu.VMEM((8, 128), F32),
        ]
        + sems(24),
        compiler_params=params(3),
        name="totals",
    )(tile)
    log_all = jnp.log(totals[:, :4])
    mask_all = loss_mask.reshape(4, 2, 128).transpose(1, 0, 2).astype(F32)
    mean_loss = jnp.sum(mask_all * (log_all - totals[:, 4:])) / token_total
    log_total = lax.dynamic_index_in_dim(log_all, core, 0, keepdims=False).reshape(512)
    wide_grad = mask[:, None] * (jnp.exp(logits - log_total[:, None]) - is_target.astype(F32))
    logit_grad = wide_grad.astype(BF16)
    scaled_grad = (wide_grad * row_scale).astype(BF16)
    scaled_grad = scaled_grad.reshape(512, 2, 512).transpose(1, 2, 0)

    normed_part = pl.pallas_call(
        normed_kernel,
        grid=(4,),
        out_shape=shape((4, 512, 1792), BF16),
        in_specs=[fixed, head_block, head_block],
        out_specs=block,
        compiler_params=plain(),
        name="normed",
    )(logit_grad, head, head_sib)

    own_scale = lax.dynamic_index_in_dim(scales, x, 0, keepdims=False)[0][:, None]
    proj_grad, gain_grad, rows_sib, grad_sib = pl.pallas_call(
        grad_kernel,
        out_shape=[
            shape((4, 2, 128, 448), BF16), shape((1, 448), F32),
            shape((4, 4, 4, 32, 1792), BF16), shape((512, 512), BF16),
        ],
        in_specs=[VMEM, VMEM, VMEM, VMEM, ANY, ANY],
        out_specs=[VMEM, VMEM, ANY, ANY],
        scratch_shapes=reduce_scratch()
        + [
            pltpu.VMEM((32, 1792), F32),
            pltpu.VMEM((4, 32, 448), F32),
            pltpu.VMEM((4, 32, 448), F32),
            pltpu.VMEM((16, 8, 128), F32),
            pltpu.VMEM((8, 128), F32),
            pltpu.VMEM((8, 8, 448), F32),
            pltpu.VMEM((8, 448), F32),
        ]
        + sems(96),
        compiler_params=params(4),
        name="grad",
    )(
        normed_part.reshape(4, 4, 4, 32, 1792), projected, final_gain[None, :], own_scale,
        rows, scaled_grad,
    )
    proj_grad = proj_grad.reshape(1024, 448)

    grad_head = pl.pallas_call(
        head_kernel,
        grid=(4,),
        out_shape=shape(head.shape, BF16),
        in_specs=[
            pl.BlockSpec((512, 512), lambda i: (0, 0)), pl.BlockSpec((512, 512), lambda i: (0, 0)),
            block, block,
        ],
        out_specs=head_block,
        compiler_params=plain(),
        name="head_grad",
    )(scaled_grad[0], grad_sib, gathered, rows_sib.reshape(4, 512, 1792))

    grad_proj_hidden = contract_first(hidden_cols, proj_grad).astype(BF16)
    grad_proj_embed = contract_first(embed_cols, proj_grad).astype(BF16)
    back = jnp.stack(
        [
            contract_last(proj_grad, proj_hidden).astype(BF16),
            contract_last(proj_grad, proj_embed).astype(BF16),
        ]
    )
    start = v * 448
    inputs = jnp.stack(
        [
            lax.dynamic_slice_in_dim(hidden_state, start, 448, 1),
            lax.dynamic_slice_in_dim(embedded_next, start, 448, 1),
        ]
    )
    gains = jnp.stack(
        [
            lax.dynamic_slice_in_dim(gain_hidden, start, 448, 0),
            lax.dynamic_slice_in_dim(gain_embed, start, 448, 0),
        ]
    )[:, None, :]
    in_scales = jnp.stack(
        [scale_of(hidden_state.astype(F32)), scale_of(embedded_next.astype(F32))]
    )

    def ring_scratch(halves, wholes, out=None):
        return [
            pltpu.VMEM((2, *halves), BF16), pltpu.VMEM((2, *wholes), BF16),
            pltpu.VMEM((2, *halves), BF16),
        ] + ([pltpu.VMEM(wholes, BF16)] if out else [])

    grads, gain_grads = pl.pallas_call(
        back_kernel,
        out_shape=[shape((2, 128, 448), BF16), shape((2, 8, 448), F32)],
        in_specs=[VMEM] * 4,
        out_specs=[VMEM] * 2,
        scratch_shapes=ring_scratch((4, 4, 16, 896), (8, 4, 16, 896), True)
        + ring_scratch((2, 4, 2, 16, 896), (2, 8, 2, 16, 896), True)
        + ring_scratch((4, 16, 896), (8, 16, 896))
        + ring_scratch((4, 16, 896), (8, 16, 896))
        + [
            pltpu.VMEM((8, 16, 896), F32),
            pltpu.VMEM((2, 8, 16, 448), BF16),
            pltpu.VMEM((2, 128, 448), BF16),
            pltpu.VMEM((2, 8, 128), F32),
            pltpu.VMEM((16, 2, 8, 128), F32),
            pltpu.VMEM((2, 8, 448), F32),
            pltpu.VMEM((8, 2, 8, 448), F32),
        ]
        + sems(48)
        + sems(16),
        compiler_params=params(5),
        name="back",
    )(back.reshape(2, 8, 2, 4, 16, 896), inputs, gains, in_scales)

    return (
        mean_loss, grads[0], grads[1], gain_grads[0, 0], gain_grads[1, 0],
        grad_proj_hidden, grad_proj_embed, gain_grad[0], grad_head,
    )


def solution(mesh):
    in_specs = (
        P("ctx", None), P("ctx", None), P(), P(), P("ctx", "vocab"), P("ctx", "vocab"),
        P("vocab"), P(("ctx", "vocab"), None), P(), P(),
    )
    out_specs = (
        P(), P("ctx", "vocab"), P("ctx", "vocab"), P("vocab"), P("vocab"),
        P("ctx", "vocab"), P("ctx", "vocab"), P("vocab"), P(("ctx", "vocab"), None),
    )
    return jax.shard_map(local, mesh=mesh, in_specs=in_specs, out_specs=out_specs, check_vma=False)
```

time: 828 us -> 330 us (0.40)
  waiting for transfers between devices: 446 us -> 0 us
  Pallas kernels: 0 us -> 281 us
  blocking collectives: 248 us -> 0 us
  matrix products: 54.3 us -> 11.6 us
  other arithmetic: 29.6 us -> 15.6 us
  between operations: 16.2 us -> 2.71 us
  starting transfers between devices: 10.4 us -> 0 us
    pallas_call x0 -> x8, Pallas kernels: none -> 281 us  [the longest x1 69.8 us: local(): pl.pallas_call(grad_kernel, out_shape=[shape((4, 2, 128, 448), BF16), sha...]
    psum x5 -> x0, blocking collectives: 185 us -> none  [the longest x1 64.9 us: local(): lax.psum((exp_part, target_part), ('ctx', 'vocab'))]
    reduce_scatter x3 -> x0, waiting for transfers between devices: 184 us -> none  [the longest x1 99.1 us: local(): lax.psum_scatter(normed_part.astype(jnp.bfloat16), 'vocab', scatter_dimen...]
    psum x2 -> x0, waiting for transfers between devices: 125 us -> none  [the longest x1 63.6 us: local(): projected = lax.psum(partial_proj, 'ctx')]
    all_gather x1 -> x0, waiting for transfers between devices: 103 us -> none  [local(): normed_rows = lax.all_gather(normed_piece, 'vocab', axis=1, tiled=True)]
    all_to_all x2 -> x0, blocking collectives: 62.9 us -> none  [the longest x1 35.8 us: local(): lax.all_to_all(hidden_part.astype(jnp.bfloat16), 'ctx', split_axis=0, con...]
    all_to_all x2 -> x0, waiting for transfers between devices: 34.2 us -> none  [the longest x1 19.8 us: local(): lax.all_to_all(normed_embed, 'ctx', split_axis=1, concat_axis=0, tiled=True)]
    dot_general x3 -> x2, matrix products: 19.3 us -> 2.29 us  [the longest x1 1.15 us: local(): jnp.dot(embed_cols, proj_embed, preferred_element_type=F32)]
  transfers between devices with their start and end apart: 8 -> 0, of which waited for: 8 -> 0; matrix products, arithmetic and copies ran while one was open for 5% -> 0% of each run, Pallas kernels for 0% -> 0%
where the time goes in v1:
time: 330 us; the launch traced here: 329 us
  Pallas kernels  281 us (85%)
  local copies, waits for them, and re-layouts  18 us (5%)
  other arithmetic  15.6 us (5%)
  matrix products  11.6 us (4%)
    pallas_call x1, Pallas kernels, local(): pl.pallas_call(grad_kernel, out_shape=[shape((4, 2, 128, 448), BF16), sha...  69.8 us
    pallas_call x1, Pallas kernels, local(): pl.pallas_call(rows_kernel, out_shape=[shape((128, 448), F32), shape((4,...  64 us
    pallas_call x1, Pallas kernels, local(): pl.pallas_call(back_kernel, out_shape=[shape((2, 128, 448), BF16), shape(...  49.8 us
    pallas_call x1, Pallas kernels, local(): pl.pallas_call(columns_kernel, out_shape=[shape((2, 8, 2, 4, 16, 896), BF...  41.3 us
    pallas_call x1, Pallas kernels, local(): pl.pallas_call(totals_kernel, out_shape=shape((2, 8, 128), F32), in_specs...  18 us
    pallas_call x1, Pallas kernels, local(): pl.pallas_call(logits_kernel, grid=(4,), out_shape=shape((512, 1024), F32...  13.1 us
    pallas_call x1, Pallas kernels, local(): pl.pallas_call(normed_kernel, grid=(4,), out_shape=shape((4, 512, 1792),...  12.8 us
    pallas_call x1, Pallas kernels, local(): pl.pallas_call(head_kernel, grid=(4,), out_shape=shape(head.shape, BF16),...  12.7 us

profile of v1, /device:TPU:1, one launch (start us, length us, event | category | flops | bytes accessed | tf_op | source)
XLA Modules:
  0.0 329.4 jit_solution(9759030237731397223)
XLA Ops:
  0.6 0.0 copy-start
  0.7 0.8 broadcast_select_fusion
  1.5 1.2 fusion.4
  2.7 1.2 fusion.6
  3.9 0.7 copy.59
  4.6 41.3 %columns.1 = (bf16[2,8,2,4,16,896]{5,4,3,2,1,0:T(8,128)(2,1)}, bf16[512,7168]{1,0:T(8,128)(2,1)}) custom-call(bf16[8,16,896]{2,1,0:T(8,128)(2,1)} %bitcast.80, bf16[512,7168]{1,0:T(8,128)(2,1)} %own.3), custom_call_target="tpu_custom_call" | custom-call | tf_op jit(solution)/shard_map/columns/pallas_call | solution.py:679
  45.9 2.5 fusion.8
  48.5 1.1 fusion.10
  49.7 0.1 copy-done.7
  49.7 0.5 copy-done.5
  50.3 1.2 convolution_add_fusion
  51.4 1.8 copy.47
  53.2 64.0 %rows.1 = (f32[128,448]{1,0:T(8,128)}, f32[4,8,128]{2,1,0:T(8,128)}, bf16[4,4,4,32,1792]{4,3,2,1,0:T(8,128)(2,1)}) custom-call(f32[4,2,128,448]{3,2,1,0:T(8,128)} %bitcast.69, f32[1,448]{1,0:T(1,128)} %bitcast.88), custom_call_target="tpu_custom_call" | custom-call | tf_op jit(solution)/shard_map/rows/pallas_call | solution.py:694
  117.3 13.1 %logits.1 = f32[512,1024]{1,0:T(8,128)} custom-call(bf16[4,512,1792]{2,1,0:T(8,128)(2,1)} %bitcast.66, bf16[512,7168]{1,0:T(8,128)(2,1)} %own.3, bf16[512,7168]{1,0:T(8,128)(2,1)} %get-tuple-element.22.sib), custom_call_target="tpu_custom_call" | custom-call | tf_op jit(solution)/shard_map/logits/pallas_call | solution.py:724
  130.4 0.9 slice.36
  131.3 2.3 exponential_reduce_fusion
  133.6 0.6 pad_maximum_fusion.3.tile
  134.2 18.0 %totals.1 = f32[2,8,128]{2,1,0:T(8,128)} custom-call(f32[8,128]{1,0:T(8,128)} %pad_maximum_fusion.3.tile), custom_call_target="tpu_custom_call" | custom-call | tf_op jit(solution)/shard_map/totals/pallas_call | solution.py:748
  152.2 1.4 slice_log_fusion
  154.2 2.1 multiply_convert_fusion
  156.3 12.8 %normed.1 = bf16[4,512,1792]{2,1,0:T(8,128)(2,1)} custom-call(bf16[512,1024]{1,0:T(8,128)(2,1)} %get-tuple-element.72.grad, bf16[512,7168]{1,0:T(8,128)(2,1)} %own.3, bf16[512,7168]{1,0:T(8,128)(2,1)} %get-tuple-element.22.sib), custom_call_target="tpu_custom_call" | custom-call | tf_op jit(solution)/shard_map/normed/pallas_call | solution.py:769
  169.1 0.7 constant_dynamic-slice_fusion
  169.8 0.7 copy.49.scale
  170.5 1.3 copy.48
  171.8 69.8 %grad.1 = (bf16[4,2,128,448]{3,2,1,0:T(8,128)(2,1)}, f32[1,448]{1,0:T(1,128)}, bf16[4,4,4,32,1792]{4,3,2,1,0:T(8,128)(2,1)}, bf16[512,512]{1,0:T(8,128)(2,1)}) custom-call(bf16[4,4,4,32,1792]{4,3,2,1,0:T(8,128)(2,1)} %bitcast.68, f32[128,448]{1,0:T(8,128)} %get-tuple-element.24.projected, f32[1,448]{1,0:T(1,128)} %bitcast.89, f32[128,1]{1,0:T(8,128)} %copy.49.scale, ...), custom_call_target="tpu_custom_call" | custom-call | tf_op jit(solution)/shard_map/grad/pallas_call | solution.py:780
  241.7 2.6 convolution_convert_fusion
  244.3 1.2 convolution_convert_fusion.1
  245.6 2.2 pad_maximum_fusion.terms
  247.8 1.1 dynamic-slice_bitcast_fusion
  248.8 0.7 pad_maximum_fusion.1.inputs
  249.6 0.8 dynamic_slice.42
  250.3 0.8 dynamic_slice.41
  251.1 0.6 broadcast_in_dim.10.gains
  251.7 0.4 multiply_reduce_fusion
  252.2 0.1 copy.51
  252.3 1.9 multiply_reduce_fusion.1
  254.2 0.1 copy.50
  254.4 0.7 pad_maximum_fusion.2.scales
  255.0 49.8 %back.1 = (bf16[2,128,448]{2,1,0:T(8,128)(2,1)}, f32[2,8,448]{2,1,0:T(8,128)}) custom-call(bf16[2,8,2,4,16,896]{5,4,3,2,1,0:T(8,128)(2,1)} %pad_maximum_fusion.terms, bf16[2,128,448]{2,1,0:T(8,128)(2,1)} %pad_maximum_fusion.1.inputs, f32[2,1,448]{2,1,0:T(1,128)} %broadcast_in_dim.10.gains, f32[2,128,1]{2,1,0:T(8,128)} %pad_maximum_fusion.2.scales), custom_call_target="tpu_custom_call" | custom-call | tf_op jit(solution)/shard_map/back/pallas_call | solution.py:851
  304.8 1.0 slice_bitcast_fusion.1
  305.8 0.8 copy.52
  306.6 0.8 copy.53
  307.3 1.3 fusion.9
  308.7 3.4 %convolution_convert_fusion.3 = bf16[896,448]{0,1:T(8,128)(2,1)} fusion(bf16[1024,896]{1,0:T(8,128)(2,1)S(1)} %bitcast.76, bf16[1024,448]{1,0:T(8,128)(2,1)} %bitcast.99), kind=kOutput, calls=%fused_computation.14 | convolution fusion | flops 822484992 | bytes 3555328 | tf_op jit(solution)/shard_map/dot_general | solution.py:649
  312.1 2.1 convolution_convert_fusion.2
  314.2 0.8 slice_bitcast_fusion.own_grad
  315.0 12.7 %head_grad.1 = bf16[512,7168]{1,0:T(8,128)(2,1)} custom-call(bf16[512,512]{1,0:T(8,128)(2,1)} %slice_bitcast_fusion.own_grad, bf16[512,512]{1,0:T(8,128)(2,1)} %get-tuple-element.29.sib_grad, bf16[4,512,1792]{2,1,0:T(8,128)(2,1)} %bitcast.67, bf16[4,512,1792]{2,1,0:T(8,128)(2,1)} %bitcast.70), custom_call_target="tpu_custom_call" | custom-call | tf_op jit(solution)/shard_map/head_grad/pallas_call | solution.py:807
  327.7 0.6 copy.61
  (38 shorter events, 0.1 us)
Async XLA Ops:
  0.6 49.6 %copy-start = (bf16[896,448]{0,1:T(8,128)(2,1)S(1)}, bf16[896,448]{0,1:T(8,128)(2,1)}, u32[]{:S(2)}) copy-start(bf16[896,448]{0,1:T(8,128)(2,1)} %param.15) | copy-start | bytes 2408452
  45.9 2.6 copy-start.14
  48.5 1.3 copy-start.7
  48.5 1.8 copy-start.5
  117.2 14.0 %copy-start.9 = (s32[1024]{0:T(1024)S(1)}, s32[1024]{0:T(1024)}, u32[]{:S(2)}) copy-start(s32[1024]{0:T(1024)} %param.19) | copy-start | bytes 12292
  117.3 14.0 %copy-start.11 = (s32[1024]{0:T(1024)S(1)}, s32[1024]{0:T(1024)}, u32[]{:S(2)}) copy-start(s32[1024]{0:T(1024)} %param.18) | copy-start | bytes 12292
  130.4 23.9 %copy-start.1 = (f32[512,1024]{1,0:T(8,128)S(1)}, f32[512,1024]{1,0:T(8,128)}, u32[]{:S(2)}) copy-start(f32[512,1024]{1,0:T(8,128)} %logits.1) | copy-start | bytes 6291460
  156.3 14.2 %copy-start.3 = (bf16[512,1024]{1,0:T(8,128)(2,1)S(1)}, bf16[512,1024]{1,0:T(8,128)(2,1)}, u32[]{:S(2)}) copy-start(bf16[512,1024]{1,0:T(8,128)(2,1)} %get-tuple-element.71) | copy-start | bytes 3145732
  241.6 2.6 copy-start.12
  241.7 2.6 copy-start.15
  245.5 2.2 copy-start.4
  255.0 53.6 %copy-start.8 = (bf16[1,8,2,4,16,896]{5,4,3,2,1,0:T(8,128)(2,1)S(1)}, bf16[1,8,2,4,16,896]{5,4,3,2,1,0:T(8,128)(2,1)}, u32[]{:S(2)}) copy-start(bf16[1,8,2,4,16,896]{5,4,3,2,1,0:T(8,128)(2,1)} %copy-done.7) | copy-start | bytes 5505028
  308.7 3.4 %copy-start.6 = (bf16[1,8,2,4,16,896]{5,4,3,2,1,0:T(8,128)(2,1)S(1)}, bf16[1,8,2,4,16,896]{5,4,3,2,1,0:T(8,128)(2,1)}, u32[]{:S(2)}) copy-start(bf16[1,8,2,4,16,896]{5,4,3,2,1,0:T(8,128)(2,1)} %copy-done.5) | copy-start | bytes 5505028
  308.7 3.4 %copy-start.13 = (bf16[4,2,128,448]{3,2,1,0:T(8,128)(2,1)S(1)}, bf16[4,2,128,448]{3,2,1,0:T(8,128)(2,1)}, u32[]{:S(2)}) copy-start(bf16[4,2,128,448]{3,2,1,0:T(8,128)(2,1)} %get-tuple-element.25) | copy-start | bytes 2752516
  312.1 2.1 copy-start.2
  315.0 12.7 %copy-start.10 = (f32[1,448]{1,0:T(1,128)S(1)}, f32[1,448]{1,0:T(1,128)}, u32[]{:S(2)}) copy-start(f32[1,448]{1,0:T(1,128)} %get-tuple-element.28) | copy-start | bytes 5380

commit v2 on v1

--- a/solution.py
+++ b/solution.py
@@ -13,7 +13,14 @@
 ANY = pl.BlockSpec(memory_space=pl.ANY)
 F32 = jnp.float32
 BF16 = jnp.bfloat16
-PARTS = ((0, 640, "xyz"), (640, 640, "yzx"), (1280, 512, "zxy"))
+PARTS = (
+    (0, 384, "xyz"),
+    (640, 384, "yzx"),
+    (1280, 256, "zxy"),
+    (384, 256, "xyz"),
+    (1024, 256, "yzx"),
+    (1536, 256, "zxy"),
+)
 
 
 class Place:
@@ -49,6 +56,7 @@
         self.send, self.recv, self.count, self.started = send, recv, 0, []
 
     def go(self, src, dst, device):
+        assert self.count < self.send.shape[0]
         copy = pltpu.make_async_remote_copy(
             src_ref=src,
             dst_ref=dst,
@@ -221,25 +229,60 @@
     copies.finish()
 
 
-def rows_kernel(
-    partial, gain, projected, scales, rows,
-    sib, summed, one, two, held, squares, mine_sq, piece, pieces, block, send, recv, local_sem,
+def all_sum(copies, here, tile, group, line, out):
+    group[here.v] = tile[...]
+    ins = [copies.go(tile, group.at[here.v], here.v_peer(o)) for o in range(1, 16)]
+    yield
+    for copy in ins:
+        copy.wait_recv()
+    x = here.c["x"]
+    line[x] = jnp.sum(group[...], axis=0)
+    ins = [copies.go(line.at[x], line.at[x], here.along("x", o)) for o in (1, 2, 3)]
+    yield
+    for copy in ins:
+        copy.wait_recv()
+    out[...] = jnp.sum(line[...], axis=0)
+
+
+def spread(row):
+    return jnp.broadcast_to(row, (128, 128)).T
+
+
+def lanes(values):
+    total = jnp.sum(values.T, axis=0, keepdims=True)
+    return [total[:, i * 128 : (i + 1) * 128] for i in range(4)]
+
+
+def reduce_name(n, k, what):
+    return f"{what}{n}{k}"
+
+
+def middle_kernel(
+    partial, gain, head_own, head_sib, position, mask, mask_row,
+    proj_grad, gain_grad, loss, rows_own, rows_sib, lgr_own, lgr_sib, r, send, recv, local_sem,
 ):
     here = Place()
     copies = Copies(send, recv)
-    rings = [here.along(a, s) for a in "xyz" for s in (1, -1)]
     greet(
-        rings
-        + [here.sibling()]
+        [here.along(a, s) for a in "xyz" for s in (1, -1)]
+        + [here.along("x", 2)]
         + [here.v_peer(o) for o in range(1, 16)]
-        + [here.along(a, 2) for a in "x"]
+        + [here.ctx_peer(o) for o in range(1, 8)]
     )
     width = 7168
-    x, y, z = here.c["x"], here.c["y"], here.c["z"]
-    swap = copies.go(partial.at[:, 1 - here.core], sib, here.sibling())
+    x, y, z, core = here.c["x"], here.c["y"], here.c["z"], here.core
+    head, rows = r["head"], r["rows"]
+    loads = [
+        pltpu.make_async_copy(head_own, head.at[pl.ds(0, 512)], local_sem.at[0]),
+        pltpu.make_async_copy(head_sib, head.at[pl.ds(512, 512)], local_sem.at[1]),
+    ]
+    swap = copies.go(partial.at[:, 1 - core], r["sib"], here.sibling())
+    for load in loads:
+        load.start()
     swap.wait_recv()
+    summed, two = r["summed"], r["two"]
     for i in range(4):
-        summed[i] = partial[i, here.core] + sib[i]
+        summed[i] = partial[i, core] + r["sib"][i]
 
     def half(ref, h):
         return ref.at[pl.ds(h * 64, 64)]
@@ -247,33 +290,29 @@
     run(
         reduce_ring(
             copies, here, "x",
-            lambda i, h: half(summed.at[i], h), half, one, two, held,
+            lambda i, h: half(summed.at[i], h), half, r["one"], two, r["held"],
             lambda out, terms: out.__setitem__(..., terms[0][...] + terms[1][...]),
         )
     )
     total = summed[x] + two[0] + two[1]
-    projected[...] = total
-    mine_sq[...] = lax.dot_general(
-        jnp.ones((8, total.shape[1]), F32), total * total, (((1,), (1,)), ((), ())),
-        precision=lax.Precision.HIGHEST, preferred_element_type=F32,
-    )
+    r["projected"][...] = total
+    piece, pieces = r["piece"], r["pieces"]
     piece[...] = (total * gain[...]).astype(BF16).reshape(piece.shape)
     exchange = []
     for o in range(1, 4):
         to = lax.rem(z + o, 4)
         exchange.append(copies.go(piece.at[to], pieces.at[z], here.along("z", o)))
-    sq_in = []
-    for o in range(1, 16):
-        sq_in.append(copies.go(mine_sq, squares.at[here.v], here.v_peer(o)))
-    squares[here.v] = mine_sq[...]
     pieces[z] = piece[z]
+    r["square"][...] = lax.dot_general(
+        jnp.ones((8, total.shape[1]), F32), total * total, (((1,), (1,)), ((), ())),
+        precision=lax.Precision.HIGHEST, preferred_element_type=F32,
+    )
+    squares, scales = r["squares"], r["scales"]
+    squares[here.v] = r["square"][...]
     for copy in exchange:
         copy.wait_recv()
     for i in range(4):
-        block[:, i * 448 : (i + 1) * 448] = pieces[i]
-    own = pltpu.make_async_copy(block, rows.at[y, x, z], local_sem)
-    own.start()
-    own.wait()
+        rows[y, x, z, :, i * 448 : (i + 1) * 448] = pieces[i]
 
     def stage(part, k):
         off, w, order = part
@@ -289,70 +328,77 @@
         return lambda: gather_ring(copies, here, order[k], slab)
 
     def scale():
+        ins = [copies.go(r["square"], squares.at[here.v], here.v_peer(o)) for o in range(1, 16)]
         yield
-        for copy in sq_in:
+        yield
+        for copy in ins:
             copy.wait_recv()
         scales[x] = lax.rsqrt(jnp.sum(squares[...], axis=0) / width + EPSILON)
-        out = [copies.go(scales.at[x], scales.at[x], here.along("x", o)) for o in range(1, 4)]
+        ins = [copies.go(scales.at[x], scales.at[x], here.along("x", o)) for o in range(1, 4)]
         yield
         yield
-        for copy in out:
+        for copy in ins:
             copy.wait_recv()
 
     run(*[chain(*[stage(part, k) for k in range(3)]) for part in PARTS], scale())
-    copies.finish()
-
-
-def totals_kernel(tile, out, group, line, part, send, recv):
-    here = Place()
-    copies = Copies(send, recv)
-    greet(
-        [here.v_peer(o) for o in range(1, 16)]
-        + [here.along("x", o) for o in (1, 2, 3)]
-        + [here.sibling()]
-    )
-    group[here.v] = tile[...]
-    ins = [copies.go(tile, group.at[here.v], here.v_peer(o)) for o in range(1, 16)]
-    for copy in ins:
-        copy.wait_recv()
-    x = here.c["x"]
-    line[x] = jnp.sum(group[...], axis=0)
-    ins = [copies.go(line.at[x], line.at[x], here.along("x", o)) for o in (1, 2, 3)]
-    for copy in ins:
-        copy.wait_recv()
-    out[here.core] = jnp.sum(line[...], axis=0)
-    copies.go(out.at[here.core], out.at[here.core], here.sibling()).wait_recv()
-    copies.finish()
-
-
-def drop(shape, axes, axis):
-    return tuple(n for n, a in zip(shape, axes) if a != axis)
-
-
-def grad_kernel(
-    terms, projected, gain, scale, rows, lgr,
-    proj_grad, gain_grad, rows_sib, lgr_sib, *scratch,
-):
-    rings_scratch, (whole, piece, pieces, dots, mine_dot, gains, mine_gain, send, recv) = (
-        scratch[:-9],
-        scratch[-9:],
-    )
-    here = Place()
-    copies = Copies(send, recv)
-    greet(
-        [here.along(a, s) for a in "xyz" for s in (1, -1)]
-        + [here.along("z", 2)]
-        + [here.v_peer(o) for o in range(1, 16)]
-        + [here.ctx_peer(o) for o in range(1, 8)]
-    )
-    width = 7168
-    z = here.c["z"]
-    swaps = [
-        copies.go(lgr.at[1], lgr_sib, here.sibling()),
-        copies.go(rows, rows_sib, here.sibling()),
-    ]
-
-    def half(ref, h):
+
+    for load in loads:
+        load.wait()
+    keep = pltpu.make_async_copy(rows, rows_own, local_sem.at[2])
+    keep.start()
+    swap_rows = copies.go(rows, rows_sib, here.sibling())
+    raw = r["raw"]
+    raw[...] = jnp.zeros_like(raw)
+
+    @pl.loop(0, 4)
+    def _(j):
+        raw[...] += lax.dot_general(
+            rows[j].reshape(512, 1792), head[:, pl.ds(pl.multiple_of(j * 1792, 128), 1792)],
+            (((1,), (1,)), ((), ())), preferred_element_type=F32,
+        )
+
+    scale_wide, log_wide = r["scale_wide"], r["log_wide"]
+    for i in range(4):
+        scale_wide[i * 128 : (i + 1) * 128] = spread(scales[i, :1])
+    column = lax.broadcasted_iota(jnp.int32, (512, 128), 1)
+    exps = jnp.zeros((512, 128), F32)
+    hits = jnp.zeros((512, 128), F32)
+    for j in range(8):
+        logit = raw[:, j * 128 : (j + 1) * 128] * scale_wide[...]
+        exps = exps + jnp.exp(logit)
+        hits = hits + jnp.where(position[...] == column + j * 128, logit, 0.0)
+    tile, sums = r["tile"], r["sums"]
+    for i, row in enumerate(lanes(exps) + lanes(hits)):
+        tile[i : i + 1] = row
+    run(all_sum(copies, here, tile, r["group"], r["line"], sums))
+    logs = jnp.log(sums[:4])
+    for i in range(4):
+        log_wide[i * 128 : (i + 1) * 128] = spread(logs[i : i + 1])
+    lost = jnp.sum(mask_row[...] * (logs - sums[4:]), axis=(0, 1), keepdims=True)
+    loss[core] = jnp.broadcast_to(lost, (8, 128))
+    swap_loss = copies.go(loss.at[core], loss.at[core], here.sibling())
+    grad, grad_t = r["grad"], r["grad_t"]
+    dots = jnp.zeros((512, 128), F32)
+    for j in range(8):
+        term = raw[:, j * 128 : (j + 1) * 128]
+        prob = jnp.exp(term * scale_wide[...] - log_wide[...])
+        hit = (position[...] == column + j * 128).astype(F32)
+        wide = mask[...] * (prob - hit)
+        rounded = wide.astype(BF16)
+        grad[:, j * 128 : (j + 1) * 128] = rounded
+        dots = dots + rounded.astype(F32) * term
+        grad_t[j * 128 : (j + 1) * 128] = (wide * scale_wide[...]).T.astype(BF16)
+    dot_tile = r["dot_tile"]
+    for i, row in enumerate(lanes(dots)):
+        dot_tile[i : i + 1] = row
+        dot_tile[i + 4 : i + 5] = row
+    swap_grad = copies.go(grad_t.at[pl.ds(512, 512)], lgr_sib, here.sibling())
+    keep_grad = pltpu.make_async_copy(grad_t.at[pl.ds(0, 512)], lgr_own, local_sem.at[3])
+    keep_grad.start()
+
+    terms, whole = r["terms"], r["whole"]
+
+    def half_lines(ref, h):
         index = (slice(None),) * (len(ref.shape) - 2) + (pl.ds(h * 16, 16),)
         return ref.at[index]
 
@@ -363,7 +409,7 @@
         source = terms
         cols = pl.ds(off, w)
         for k in range(3):
-            one, two, held, out = rings_scratch[(n * 3 + k) * 4 : (n * 3 + k) * 4 + 4]
+            one, two, held = (r[reduce_name(n, k, what)] for what in ("one", "two", "held"))
             axis = order[k]
 
             def slab(i, h, source=source, axes=axes, cols=cols, axis=axis):
@@ -372,60 +418,82 @@
                 return source.at[(*index, lines, cols)]
 
             yield from reduce_ring(
-                copies, here, axis, slab, half, one, two, held, add_refs
+                copies, here, axis, slab, half_lines, one, two, held, add_refs
             )
             if k < 2:
+                out = r[reduce_name(n, k, "out")]
                 add_refs(out, (slab(here.c[axis], None), two.at[0], two.at[1]))
+                source, cols = out, slice(None)
             else:
                 own = slab(here.c[axis], None)[...].astype(F32)
                 whole[:, off : off + w] = own + two[0].astype(F32) + two[1].astype(F32)
-            source, cols = out, slice(None)
             axes = axes.replace(axis, "")
-            yield
-
-    run(*[part_rings(n, part) for n, part in enumerate(PARTS)])
+
+    def product(part):
+        off, w, _ = part
+
+        @pl.loop(0, 4)
+        def _(j):
+            terms[j, :, :, :, off : off + w] = (
+                jnp.dot(
+                    grad[...], head[:, pl.ds(pl.multiple_of(j * 1792 + off, 128), w)],
+                    preferred_element_type=F32,
+                )
+                .astype(BF16)
+                .reshape(4, 4, 32, w)
+            )
+
+    rings = []
+    for n, part in enumerate(PARTS):
+        product(part)
+        ring = part_rings(n, part)
+        next(ring)
+        rings.append(ring)
+    row_dots = all_sum(copies, here, dot_tile, r["group2"], r["line2"], r["sums2"])
+    run(*rings, row_dots)
+
+    back, backs = r["back"], r["backs"]
     for i in range(4):
-        piece[i] = whole[:, i * 448 : (i + 1) * 448]
+        back[i] = whole[:, i * 448 : (i + 1) * 448]
     exchange = []
     for o in range(1, 4):
         to = lax.rem(z + o, 4)
-        exchange.append(copies.go(piece.at[to], pieces.at[z], here.along("z", o)))
-    pieces[z] = piece[z]
+        exchange.append(copies.go(back.at[to], backs.at[z], here.along("z", o)))
+    backs[z] = back[z]
+    row_scale = scale_wide[pl.ds(pl.multiple_of(x * 128, 128), 128)][:, :1]
+    row_dot = spread(r["sums2"][pl.ds(x, 1)])[:, :1]
+    wide = r["projected"][...]
     for copy in exchange:
         copy.wait_recv()
-    normed_grad = pieces[...].reshape(128, 448)
-    wide = projected[...]
-    row_scale = scale[...]
-    scaled = normed_grad * gain[...]
-    mine_dot[...] = lax.dot_general(
-        jnp.ones((8, 448), F32), scaled * wide, (((1,), (1,)), ((), ())),
-        precision=lax.Precision.HIGHEST, preferred_element_type=F32,
-    )
-    ins = [copies.go(mine_dot, dots.at[here.v], here.v_peer(o)) for o in range(1, 16)]
-    dots[here.v] = mine_dot[...]
-    mine_gain[...] = jnp.broadcast_to(
-        jnp.sum(normed_grad * wide * row_scale, axis=0, keepdims=True), (8, 448)
-    )
-    gain_ins = [copies.go(mine_gain, gains.at[here.ctx], here.ctx_peer(o)) for o in range(1, 8)]
-    gains[here.ctx] = mine_gain[...]
-    for copy in ins:
-        copy.wait_recv()
-    row_dot = jnp.sum(dots[...], axis=0).T[:, :1]
-    grad = row_scale * scaled - wide * (row_scale * row_scale * row_scale) * (row_dot / width)
-    x, core = here.c["x"], here.core
-    proj_grad[x, core] = grad.astype(BF16)
-
-    def slab(i, h):
+    normed_grad = backs[...].reshape(128, 448)
+    grad_out = row_scale * (normed_grad * gain[...]) - wide * (
+        row_scale * row_scale * row_scale
+    ) * (row_dot / width)
+    proj_grad[x, core] = grad_out.astype(BF16)
+
+    def row_slab(i, h):
         lines = slice(None) if h is None else pl.ds(h * 64, 64)
         return proj_grad.at[i, core, lines]
 
-    run(gather_ring(copies, here, "x", slab))
+    def gain_sum():
+        mine, every = r["gain_mine"], r["gain_all"]
+        mine[...] = jnp.broadcast_to(
+            jnp.sum(normed_grad * wide * row_scale, axis=0, keepdims=True), (8, 448)
+        )
+        every[here.ctx] = mine[...]
+        ins = [copies.go(mine, every.at[here.ctx], here.ctx_peer(o)) for o in range(1, 8)]
+        yield
+        yield
+        for copy in ins:
+            copy.wait_recv()
+        gain_grad[...] = jnp.sum(every[...], axis=0)[:1]
+
+    run(gather_ring(copies, here, "x", row_slab), gain_sum())
     copies.go(proj_grad.at[:, core], proj_grad.at[:, core], here.sibling()).wait_recv()
-    for copy in gain_ins:
+    for copy in (swap_rows, swap_loss, swap_grad):
         copy.wait_recv()
-    gain_grad[...] = jnp.sum(gains[...], axis=0)[:1]
-    for copy in swaps:
-        copy.wait_recv()
+    keep.wait()
+    keep_grad.wait()
     copies.finish()
 
 
@@ -583,24 +651,6 @@
     copies.finish()
 
 
-def logits_kernel(rows, own, sib, out):
-    @pl.when(pl.program_id(0) == 0)
-    def _():
-        out[...] = jnp.zeros_like(out)
-
-    for h, head in enumerate((own, sib)):
-        out[:, h * 512 : (h + 1) * 512] += lax.dot_general(
-            rows[0], head[...], (((1,), (1,)), ((), ())), preferred_element_type=F32
-        )
-
-
-def normed_kernel(grad, own, sib, out):
-    out[0] = (
-        jnp.dot(grad[:, :512], own[...], preferred_element_type=F32)
-        + jnp.dot(grad[:, 512:], sib[...], preferred_element_type=F32)
-    ).astype(BF16)
-
-
 def head_kernel(own_grad, sib_grad, own, sib, out):
     out[...] = (
         jnp.dot(own_grad[...], own[0], preferred_element_type=F32)
@@ -626,17 +676,47 @@
     return jax.ShapeDtypeStruct(dims, kind)
 
 
-def reduce_scratch():
-    scratch = []
-    for _, w, order in PARTS:
+def middle_scratch():
+    scratch = {
+        "head": pltpu.VMEM((1024, 7168), BF16),
+        "rows": pltpu.VMEM((4, 4, 4, 32, 1792), BF16),
+        "terms": pltpu.VMEM((4, 4, 4, 32, 1792), BF16),
+        "raw": pltpu.VMEM((512, 1024), F32),
+        "grad": pltpu.VMEM((512, 1024), BF16),
+        "grad_t": pltpu.VMEM((1024, 512), BF16),
+        "scale_wide": pltpu.VMEM((512, 128), F32),
+        "log_wide": pltpu.VMEM((512, 128), F32),
+        "sib": pltpu.VMEM((4, 128, 448), F32),
+        "summed": pltpu.VMEM((4, 128, 448), F32),
+        "one": pltpu.VMEM((2, 64, 448), F32),
+        "two": pltpu.VMEM((2, 128, 448), F32),
+        "held": pltpu.VMEM((2, 64, 448), F32),
+        "projected": pltpu.VMEM((128, 448), F32),
+        "square": pltpu.VMEM((8, 128), F32),
+        "squares": pltpu.VMEM((16, 8, 128), F32),
+        "scales": pltpu.VMEM((4, 8, 128), F32),
+        "piece": pltpu.VMEM((4, 32, 448), BF16),
+        "pieces": pltpu.VMEM((4, 32, 448), BF16),
+        "back": pltpu.VMEM((4, 32, 448), F32),
+        "backs": pltpu.VMEM((4, 32, 448), F32),
+        "whole": pltpu.VMEM((32, 1792), F32),
+        "gain_mine": pltpu.VMEM((8, 448), F32),
+        "gain_all": pltpu.VMEM((8, 8, 448), F32),
+    }
+    for name in ("tile", "sums", "dot_tile", "sums2"):
+        scratch[name] = pltpu.VMEM((8, 128), F32)
+    for name in ("group", "group2"):
+        scratch[name] = pltpu.VMEM((16, 8, 128), F32)
+    for name in ("line", "line2"):
+        scratch[name] = pltpu.VMEM((4, 8, 128), F32)
+    for n, (_, w, _) in enumerate(PARTS):
         dims = (4, 4)
         for k in range(3):
-            scratch += [
-                pltpu.VMEM((2, *dims, 16, w), BF16),
-                pltpu.VMEM((2, *dims, 32, w), BF16),
-                pltpu.VMEM((2, *dims, 16, w), BF16),
-                pltpu.VMEM((*dims, 32, w), BF16),
-            ]
+            scratch[reduce_name(n, k, "one")] = pltpu.VMEM((2, *dims, 16, w), BF16)
+            scratch[reduce_name(n, k, "held")] = pltpu.VMEM((2, *dims, 16, w), BF16)
+            scratch[reduce_name(n, k, "two")] = pltpu.VMEM((2, *dims, 32, w), BF16)
+            if k < 2:
+                scratch[reduce_name(n, k, "out")] = pltpu.VMEM((*dims, 32, w), BF16)
             dims = dims[1:]
     return scratch
 
@@ -691,117 +771,37 @@
         embed_cols, proj_embed, preferred_element_type=F32
     )
 
-    projected, scales, rows = pl.pallas_call(
-        rows_kernel,
-        out_shape=[
-            shape((128, 448), F32), shape((4, 8, 128), F32), shape((4, 4, 4, 32, 1792), BF16),
-        ],
-        in_specs=[VMEM, VMEM],
-        out_specs=[VMEM, VMEM, ANY],
-        scratch_shapes=[
-            pltpu.VMEM((4, 128, 448), F32),
-            pltpu.VMEM((4, 128, 448), F32),
-            pltpu.VMEM((2, 64, 448), F32),
-            pltpu.VMEM((2, 128, 448), F32),
-            pltpu.VMEM((2, 64, 448), F32),
-            pltpu.VMEM((16, 8, 128), F32),
-            pltpu.VMEM((8, 128), F32),
-            pltpu.VMEM((4, 32, 448), BF16),
-            pltpu.VMEM((4, 32, 448), BF16),
-            pltpu.VMEM((32, 1792), BF16),
-        ]
-        + sems(72)
-        + [pltpu.SemaphoreType.DMA],
-        compiler_params=params(2),
-        name="rows",
-    )(partial.reshape(4, 2, 128, 448), final_gain[None, :])
-
-    gathered = rows.reshape(4, 512, 1792)
-    row_scale = scales[:, 0].reshape(512, 1)
+    def of_core(values, k):
+        return lax.dynamic_index_in_dim(values.reshape(4, 2, 128), k, 1, keepdims=False)
+
+    my_targets = of_core(targets, core)
+    mask_row = of_core(loss_mask, core).astype(F32)
+    own_at = my_targets - (ctx * 16 + v) * 512
+    sib_at = my_targets - ((ctx + 1 - 2 * core) * 16 + v) * 512
+    position = jnp.where(
+        (own_at >= 0) & (own_at < 512),
+        own_at,
+        jnp.where((sib_at >= 0) & (sib_at < 512), sib_at + 512, -1),
+    )
     block = pl.BlockSpec((1, 512, 1792), lambda i: (i, 0, 0))
     head_block = pl.BlockSpec((512, 1792), lambda i: (0, i))
-    fixed = pl.BlockSpec((512, 1024), lambda i: (0, 0))
-    raw_logits = pl.pallas_call(
-        logits_kernel,
-        grid=(4,),
-        out_shape=shape((512, 1024), F32),
-        in_specs=[block, head_block, head_block],
-        out_specs=fixed,
-        compiler_params=plain(),
-        name="logits",
-    )(gathered, head, head_sib)
-    logits = raw_logits * row_scale
-    own_ids = (ctx * 16 + v) * 512 + lax.iota(jnp.int32, 512)
-    sib_ids = ((ctx + 1 - 2 * core) * 16 + v) * 512 + lax.iota(jnp.int32, 512)
-    vocab_ids = jnp.concatenate([own_ids, sib_ids])
-
-    def of_core(values, k):
-        return lax.dynamic_index_in_dim(values.reshape(4, 2, 128), k, 1, keepdims=False)
-
-    my_targets = of_core(targets, core).reshape(512)
-    mask = of_core(loss_mask, core).reshape(512).astype(F32)
-    is_target = my_targets[:, None] == vocab_ids[None, :]
-    exp_part = jnp.sum(jnp.exp(logits), axis=-1)
-    target_part = jnp.sum(jnp.where(is_target, logits, F32(0.0)), axis=-1)
-    tile = jnp.concatenate([exp_part.reshape(4, 128), target_part.reshape(4, 128)])
-
-    totals = pl.pallas_call(
-        totals_kernel,
-        out_shape=shape((2, 8, 128), F32),
-        in_specs=[VMEM],
-        out_specs=VMEM,
-        scratch_shapes=[
-            pltpu.VMEM((16, 8, 128), F32), pltpu.VMEM((4, 8, 128), F32), pltpu.VMEM((8, 128), F32),
-        ]
-        + sems(24),
-        compiler_params=params(3),
-        name="totals",
-    )(tile)
-    log_all = jnp.log(totals[:, :4])
-    mask_all = loss_mask.reshape(4, 2, 128).transpose(1, 0, 2).astype(F32)
-    mean_loss = jnp.sum(mask_all * (log_all - totals[:, 4:])) / token_total
-    log_total = lax.dynamic_index_in_dim(log_all, core, 0, keepdims=False).reshape(512)
-    wide_grad = mask[:, None] * (jnp.exp(logits - log_total[:, None]) - is_target.astype(F32))
-    logit_grad = wide_grad.astype(BF16)
-    scaled_grad = (wide_grad * row_scale).astype(BF16)
-    scaled_grad = scaled_grad.reshape(512, 2, 512).transpose(1, 2, 0)
-
-    normed_part = pl.pallas_call(
-        normed_kernel,
-        grid=(4,),
-        out_shape=shape((4, 512, 1792), BF16),
-        in_specs=[fixed, head_block, head_block],
-        out_specs=block,
-        compiler_params=plain(),
-        name="normed",
-    )(logit_grad, head, head_sib)
-
-    own_scale = lax.dynamic_index_in_dim(scales, x, 0, keepdims=False)[0][:, None]
-    proj_grad, gain_grad, rows_sib, grad_sib = pl.pallas_call(
-        grad_kernel,
+    proj_grad, gain_grad, loss, rows_own, rows_sib, lgr_own, lgr_sib = pl.pallas_call(
+        middle_kernel,
         out_shape=[
-            shape((4, 2, 128, 448), BF16), shape((1, 448), F32),
-            shape((4, 4, 4, 32, 1792), BF16), shape((512, 512), BF16),
+            shape((4, 2, 128, 448), BF16), shape((1, 448), F32), shape((2, 8, 128), F32),
+            shape((4, 4, 4, 32, 1792), BF16), shape((4, 4, 4, 32, 1792), BF16),
+            shape((512, 512), BF16), shape((512, 512), BF16),
         ],
-        in_specs=[VMEM, VMEM, VMEM, VMEM, ANY, ANY],
-        out_specs=[VMEM, VMEM, ANY, ANY],
-        scratch_shapes=reduce_scratch()
-        + [
-            pltpu.VMEM((32, 1792), F32),
-            pltpu.VMEM((4, 32, 448), F32),
-            pltpu.VMEM((4, 32, 448), F32),
-            pltpu.VMEM((16, 8, 128), F32),
-            pltpu.VMEM((8, 128), F32),
-            pltpu.VMEM((8, 8, 448), F32),
-            pltpu.VMEM((8, 448), F32),
-        ]
-        + sems(96),
-        compiler_params=params(4),
-        name="grad",
+        in_specs=[VMEM, VMEM, ANY, ANY, VMEM, VMEM, VMEM],
+        out_specs=[VMEM, VMEM, VMEM, ANY, ANY, ANY, ANY],
+        scratch_shapes=[middle_scratch()] + sems(264) + [pltpu.SemaphoreType.DMA((4,))],
+        compiler_params=params(2, 60),
+        name="middle",
     )(
-        normed_part.reshape(4, 4, 4, 32, 1792), projected, final_gain[None, :], own_scale,
-        rows, scaled_grad,
-    )
+        partial.reshape(4, 2, 128, 448), final_gain[None, :], head, head_sib,
+        position.reshape(512, 1), mask_row.reshape(512, 1), mask_row,
+    )
+    mean_loss = (loss[0, 0, 0] + loss[1, 0, 0]) / token_total
     proj_grad = proj_grad.reshape(1024, 448)
 
     grad_head = pl.pallas_call(
@@ -815,7 +815,7 @@
         out_specs=head_block,
         compiler_params=plain(),
         name="head_grad",
-    )(scaled_grad[0], grad_sib, gathered, rows_sib.reshape(4, 512, 1792))
+    )(lgr_own, lgr_sib, rows_own.reshape(4, 512, 1792), rows_sib.reshape(4, 512, 1792))
 
     grad_proj_hidden = contract_first(hidden_cols, proj_grad).astype(BF16)
     grad_proj_embed = contract_first(embed_cols, proj_grad).astype(BF16)

time: 330 us -> 293 us (0.89)
  Pallas kernels: 281 us -> 251 us
  other arithmetic: 15.6 us -> 10.6 us
    pallas_call x5 -> x1, Pallas kernels: 178 us -> 145 us  [local(): pl.pallas_call(middle_kernel, out_shape=[shape((4, 2, 128, 448), BF16), s...]
where the time goes in v2:
time: 293 us; the launch traced here: 292 us
  Pallas kernels  251 us (86%)
  local copies, waits for them, and re-layouts  16.9 us (6%)
  other arithmetic  10.6 us (4%)
  matrix products  10.2 us (3%)
  between operations  3.3 us (1%)
    pallas_call x1, Pallas kernels, local(): pl.pallas_call(middle_kernel, out_shape=[shape((4, 2, 128, 448), BF16), s...  145 us
    pallas_call x1, Pallas kernels, local(): pl.pallas_call(back_kernel, out_shape=[shape((2, 128, 448), BF16), shape(...  51.5 us
    pallas_call x1, Pallas kernels, local(): pl.pallas_call(columns_kernel, out_shape=[shape((2, 8, 2, 4, 16, 896), BF...  41.3 us
    pallas_call x1, Pallas kernels, local(): pl.pallas_call(head_kernel, grid=(4,), out_shape=shape(head.shape, BF16),...  13 us

profile of v2, /device:TPU:1, one launch (start us, length us, event | category | flops | bytes accessed | tf_op | source)
XLA Modules:
  0.0 292.0 jit_solution(2376510308994540473)
XLA Ops:
  0.6 0.0 copy-start
  0.7 1.3 fusion
  2.0 0.8 broadcast_select_fusion
  2.8 1.2 fusion.2
  3.9 0.7 copy.65
  4.6 41.3 %columns.1 = (bf16[2,8,2,4,16,896]{5,4,3,2,1,0:T(8,128)(2,1)}, bf16[512,7168]{1,0:T(8,128)(2,1)}) custom-call(bf16[8,16,896]{2,1,0:T(8,128)(2,1)} %bitcast.66, bf16[512,7168]{1,0:T(8,128)(2,1)} %head_own.1), custom_call_target="tpu_custom_call" | custom-call | tf_op jit(solution)/shard_map/columns/pallas_call | solution.py:759
  45.9 2.5 fusion.4
  48.4 0.0 copy-start.2
  48.4 0.0 copy-done
  48.4 0.0 copy-start.8
  48.5 1.1 fusion.7
  49.6 0.1 copy-done.2
  49.7 0.5 copy-done.8
  50.2 2.4 convolution_add_fusion
  52.6 2.9 copy.51
  55.5 0.1 copy.52
  55.7 0.1 copy.55
  55.8 0.7 and_select_fusion.position
  56.6 0.9 copy.57.mask
  57.5 0.6 convert_bitcast_fusion.mask_row
  58.0 145.3 %middle.1 = (bf16[4,2,128,448]{3,2,1,0:T(8,128)(2,1)}, f32[1,448]{1,0:T(1,128)}, f32[2,8,128]{2,1,0:T(8,128)}, bf16[4,4,4,32,1792]{4,3,2,1,0:T(8,128)(2,1)}, bf1...) custom-call(f32[4,2,128,448]{3,2,1,0:T(8,128)} %bitcast.56, ...), custom_call_target="tpu_custom_call" | custom-call | tf_op jit(solution)/shard_map/middle/pallas_call | solution.py:788
  203.3 0.0 copy-start.3
  203.3 0.0 copy-start.7
  203.3 13.0 %head_grad.1 = bf16[512,7168]{1,0:T(8,128)(2,1)} custom-call(bf16[512,512]{1,0:T(8,128)(2,1)} %get-tuple-element.27.own_grad, bf16[512,512]{1,0:T(8,128)(2,1)} %get-tuple-element.28.sib_grad, bf16[4,512,1792]{2,1,0:T(8,128)(2,1)} %bitcast.57, bf16[4,512,1792]{2,1,0:T(8,128)(2,1)} %bitcast.58), custom_call_target="tpu_custom_call" | custom-call | tf_op jit(solution)/shard_map/head_grad/pallas_call | solution.py:807
  216.4 2.0 convolution_convert_fusion.2
  218.4 2.0 convolution_convert_fusion.3
  220.5 1.2 convolution_convert_fusion.1
  221.7 0.0 copy-done.9
  221.7 1.3 convolution_convert_fusion
  223.0 0.0 copy-start.1
  223.0 2.2 pad_maximum_fusion.terms
  225.2 1.1 dynamic-slice_bitcast_fusion
  226.2 0.7 pad_maximum_fusion.1.inputs
  227.0 0.8 dynamic_slice.31
  227.8 0.8 dynamic_slice.32
  228.5 0.6 broadcast_in_dim.16.gains
  229.1 0.4 multiply_reduce_fusion.1
  229.6 0.1 copy.58
  229.7 1.9 multiply_reduce_fusion
  231.7 0.1 copy.59
  231.8 0.7 pad_maximum_fusion.2.scales
  232.4 51.5 %back.1 = (bf16[2,128,448]{2,1,0:T(8,128)(2,1)}, f32[2,8,448]{2,1,0:T(8,128)}) custom-call(bf16[2,8,2,4,16,896]{5,4,3,2,1,0:T(8,128)(2,1)} %pad_maximum_fusion.terms, bf16[2,128,448]{2,1,0:T(8,128)(2,1)} %pad_maximum_fusion.1.inputs, f32[2,1,448]{2,1,0:T(1,128)} %broadcast_in_dim.16.gains, f32[2,128,1]{2,1,0:T(8,128)} %pad_maximum_fusion.2.scales), custom_call_target="tpu_custom_call" | custom-call | tf_op jit(solution)/shard_map/back/pallas_call | solution.py:851
  283.9 1.0 slice_bitcast_fusion
  284.9 0.8 copy.60
  285.7 0.8 copy.61
  286.4 1.3 fusion.5
  287.8 1.2 fusion.6
  290.3 0.6 copy.67
  (17 shorter events, 0.1 us)
Async XLA Ops:
  0.6 47.8 %copy-start = (bf16[896,448]{0,1:T(8,128)(2,1)S(1)}, bf16[896,448]{0,1:T(8,128)(2,1)}, u32[]{:S(2)}) copy-start(bf16[896,448]{0,1:T(8,128)(2,1)} %param.14) | copy-start | bytes 2408452
  48.4 1.3 copy-start.2
  48.4 1.8 copy-start.8
  52.6 2.9 copy-start.6
  52.6 3.9 %copy-start.5 = (s32[1024]{0:T(1024)S(1)}, s32[1024]{0:T(1024)}, u32[]{:S(2)}) copy-start(s32[1024]{0:T(1024)} %param.19) | copy-start | bytes 12292
  203.3 13.1 %copy-start.3 = (bf16[1,8,2,4,16,896]{5,4,3,2,1,0:T(8,128)(2,1)S(1)}, bf16[1,8,2,4,16,896]{5,4,3,2,1,0:T(8,128)(2,1)}, u32[]{:S(2)}) copy-start(bf16[1,8,2,4,16,896]{5,4,3,2,1,0:T(8,128)(2,1)} %copy-done.2) | copy-start | bytes 5505028
  203.3 13.1 %copy-start.7 = (bf16[4,2,128,448]{3,2,1,0:T(8,128)(2,1)S(1)}, bf16[4,2,128,448]{3,2,1,0:T(8,128)(2,1)}, u32[]{:S(2)}) copy-start(bf16[4,2,128,448]{3,2,1,0:T(8,128)(2,1)} %get-tuple-element.23) | copy-start | bytes 2752516
  220.5 1.3 copy-start.9
  223.0 2.2 copy-start.1
  232.4 57.8 %copy-start.4 = (f32[1,448]{1,0:T(1,128)S(1)}, f32[1,448]{1,0:T(1,128)}, u32[]{:S(2)}) copy-start(f32[1,448]{1,0:T(1,128)} %get-tuple-element.26) | copy-start | bytes 5380

commit v3 on v2

v3 whole, which is shorter than its diff:
```python
import jax
import jax.numpy as jnp
from jax import lax
from jax.experimental import pallas as pl
from jax.experimental.pallas import tpu as pltpu
from jax.sharding import PartitionSpec as P

EPSILON = 1e-06
MESH = pl.DeviceIdType.MESH
VMEM = pl.BlockSpec(memory_space=pltpu.VMEM)
ANY = pl.BlockSpec(memory_space=pl.ANY)
F32 = jnp.float32
BF16 = jnp.bfloat16
PARTS = (
    (0, 384, "xyz"),
    (384, 384, "yzx"),
    (768, 256, "zxy"),
    (1024, 256, "xyz"),
    (1280, 256, "yzx"),
    (1536, 256, "zxy"),
)
BATCHES = ((0, 1024), (1024, 768))


class Place:
    def __init__(self):
        self.ctx = lax.axis_index("ctx")
        self.v = lax.axis_index("vocab")
        self.c = {"x": self.ctx // 2, "y": self.v // 4, "z": self.v % 4}
        self.core = self.ctx % 2

    def at(self, ctx=None, v=None):
        return {"ctx": self.ctx if ctx is None else ctx, "vocab": self.v if v is None else v}

    def along(self, axis, step):
        i = lax.rem(self.c[axis] + step + 4, 4)
        if axis == "x":
            return self.at(ctx=i * 2 + self.core)
        if axis == "y":
            return self.at(v=i * 4 + self.c["z"])
        return self.at(v=self.c["y"] * 4 + i)

    def sibling(self):
        return self.at(ctx=self.c["x"] * 2 + 1 - self.core)

    def ctx_peer(self, o):
        return self.at(ctx=lax.rem(self.ctx + o, 8))

    def v_peer(self, o):
        return self.at(v=lax.rem(self.v + o, 16))


class Copies:
    def __init__(self, send, recv):
        self.send, self.recv, self.count, self.started = send, recv, 0, []

    def go(self, src, dst, device):
        assert self.count < self.send.shape[0]
        copy = pltpu.make_async_remote_copy(
            src_ref=src,
            dst_ref=dst,
            send_sem=self.send.at[self.count],
            recv_sem=self.recv.at[self.count],
            device_id=device,
            device_id_type=MESH,
        )
        self.count += 1
        copy.start()
        self.started.append(copy)
        return copy

    def finish(self):
        for copy in self.started:
            copy.wait_send()
        self.started = []


def greet(devices):
    barrier = pltpu.get_barrier_semaphore()
    for device in devices:
        pl.semaphore_signal(barrier, inc=1, device_id=device, device_id_type=MESH)


def met(devices):
    pl.semaphore_wait(pltpu.get_barrier_semaphore(), len(devices))


def run(*rings):
    rings = list(rings)
    while rings:
        left = []
        for ring in rings:
            try:
                next(ring)
                left.append(ring)
            except StopIteration:
                pass
        rings = left


def chain(*makers):
    for maker in makers:
        yield from maker()


def gather_ring(copies, here, axis, slab):
    me = here.c[axis]
    right, left = here.along(axis, 1), here.along(axis, -1)
    before, after = lax.rem(me + 3, 4), lax.rem(me + 1, 4)

    def send(i, h, device):
        return copies.go(slab(i, h), slab(i, h), device)

    right_0, left_1 = send(me, 0, right), send(me, 1, left)
    right_1, left_0 = send(me, 1, right), send(me, 0, left)
    yield
    right_0.wait_recv()
    far_a = send(before, 0, right)
    left_1.wait_recv()
    far_b = send(after, 1, left)
    yield
    for copy in (right_1, left_0, far_a, far_b):
        copy.wait_recv()


def gather_near(copies, here, axis, slab):
    me = here.c[axis]
    ins = [copies.go(slab(me, None), slab(me, None), here.along(axis, o)) for o in (1, 2, 3)]
    yield
    for copy in ins:
        copy.wait_recv()


def reduce_ring(copies, here, axis, slab, half, one, two, held, add):
    if isinstance(axis, str):
        me, right, left = here.c[axis], here.along(axis, 1), here.along(axis, -1)
    else:
        me, right, left = axis
    before, after, far = lax.rem(me + 3, 4), lax.rem(me + 1, 4), lax.rem(me + 2, 4)
    a1 = copies.go(slab(far, 0), one.at[0], right)
    b1 = copies.go(slab(far, 1), one.at[1], left)
    a2 = copies.go(slab(after, 1), half(two.at[0], 1), right)
    b2 = copies.go(slab(before, 0), half(two.at[1], 0), left)
    yield
    a1.wait_recv()
    add(held.at[0], (slab(after, 0), one.at[0]))
    a3 = copies.go(held.at[0], half(two.at[0], 0), right)
    b1.wait_recv()
    add(held.at[1], (slab(before, 1), one.at[1]))
    b3 = copies.go(held.at[1], half(two.at[1], 1), left)
    yield
    a2.wait_recv()
    b2.wait_recv()
    a3.wait_recv()
    b3.wait_recv()


def reduce_near(copies, here, axis, slab, recv, finish):
    if isinstance(axis, str):
        me, to = here.c[axis], [here.along(axis, o) for o in (1, 2, 3)]
    else:
        me, to = axis
    ins = [
        copies.go(slab(lax.rem(me + o, 4)), recv.at[o - 1], to[o - 1]) for o in (1, 2, 3)
    ]
    yield
    for copy in ins:
        copy.wait_recv()
    finish(slab(me), [recv.at[o] for o in range(3)])


def add_refs(out, terms):
    lead = out.shape[:-2]
    total = 1
    for n in lead:
        total *= n

    def block(index):
        acc = terms[0][index].astype(F32)
        for term in terms[1:]:
            acc = acc + term[index].astype(F32)
        out[index] = acc.astype(out.dtype)

    if total == 1:
        block(tuple(0 for _ in lead) + (slice(None), slice(None)))
        return

    @pl.loop(0, total)
    def _(i):
        index = []
        for n in reversed(lead):
            index.append(i % n)
            i = i // n
        block(tuple(reversed(index)) + (slice(None), slice(None)))


def all_sum(copies, here, tile, group, line, out):
    group[here.v] = tile[...]
    ins = [copies.go(tile, group.at[here.v], here.v_peer(o)) for o in range(1, 16)]
    yield
    for copy in ins:
        copy.wait_recv()
    x = here.c["x"]
    line[x] = jnp.sum(group[...], axis=0)
    ins = [copies.go(line.at[x], line.at[x], here.along("x", o)) for o in (1, 2, 3)]
    yield
    for copy in ins:
        copy.wait_recv()
    out[...] = jnp.sum(line[...], axis=0)


def spread(row):
    return jnp.broadcast_to(row, (128, 128)).T


def lanes(values):
    total = jnp.sum(values.T, axis=0, keepdims=True)
    return [total[:, i * 128 : (i + 1) * 128] for i in range(4)]


class Bag:
    def __init__(self, refs):
        self.__dict__.update(refs)


def trickle(pieces):
    for start in pieces:
        start()
        yield


def middle_kernel(
    hidden, embed, gain_h, gain_e, proj_h, proj_e, gain, head_own, targets, loss_mask,
    proj_grad, gain_grad, loss, cols_out, half_out, rows_sib, lgr_sib,
    r, send, recv, local_sem,
):
    r = Bag(r)
    here = Place()
    copies = Copies(send, recv)
    friends = [here.ctx_peer(o) for o in range(1, 8)] + [here.v_peer(o) for o in range(1, 16)]
    greet(friends)
    width = 7168
    x, y, z, core = here.c["x"], here.c["y"], here.c["z"], here.core
    head, rows, cols = r.head, r.rows, r.cols
    locals_ = []

    def bring(src, dst):
        copy = pltpu.make_async_copy(src, dst, local_sem.at[len(locals_)])
        copy.start()
        locals_.append(copy)
        return copy

    sliver = pl.ds(pl.multiple_of(lax.rem(here.v, 8) * 16, 16), 16)
    raw_in = [bring(hidden.at[sliver], r.raw_in.at[0]), bring(embed.at[sliver], r.raw_in.at[1])]
    weights = [bring(proj_h, r.weights.at[0]), bring(proj_e, r.weights.at[1])]
    load = bring(head_own, head.at[pl.ds(0, 512)])
    for copy in raw_in:
        copy.wait()
    first = here.v < 8
    normed = r.normed

    def norm(e, gains):
        wide = r.raw_in[e].astype(F32)
        scale = lax.rsqrt(jnp.mean(wide * wide, axis=-1, keepdims=True) + EPSILON)
        for c in range(8):
            part = slice(c * 896, (c + 1) * 896)
            normed[c] = (wide[:, part] * scale * gains[:, part]).astype(BF16)

    @pl.when(first)
    def _():
        norm(0, gain_h)

    @pl.when(jnp.logical_not(first))
    def _():
        norm(1, gain_e)

    met(friends)

    def sliver_at(c):
        return cols.at[y // 2, c // 2, c % 2, y % 2, z]

    arrivals = []
    for o in range(1, 8):
        peer = lax.rem(here.ctx + o, 8)
        arrivals.append(copies.go(normed.at[peer], sliver_at(here.ctx), here.ctx_peer(o)))
    cols[y // 2, x, core, y % 2, z] = normed[here.ctx]
    for arrival in arrivals:
        arrival.wait_recv()

    def col_slabs(part):
        lanes_ = pl.ds(*part)

        def span(h):
            return slice(None) if h is None else pl.ds(h * 2, 2)

        return {
            "y_first": lambda i, h: cols.at[i // 2, span(h), :, i % 2, z, :, lanes_],
            "z_last": lambda i, h: cols.at[:, span(h), :, :, i, :, lanes_],
            "z_first": lambda i, h: cols.at[y // 2, span(h), :, y % 2, i, :, lanes_],
            "y_last": lambda i, h: cols.at[i // 2, span(h), :, i % 2, :, :, lanes_],
        }

    def col_ring(part, names):
        slabs = col_slabs(part)
        return chain(
            lambda: gather_near(copies, here, names[0][0], slabs[names[0]]),
            lambda: gather_ring(copies, here, names[1][0], slabs[names[1]]),
        )

    head_pieces = []

    def head_piece(i):
        piece_rows = pl.ds(i * 128, 128)
        head_pieces.append(
            copies.go(
                head_own.at[piece_rows], head.at[pl.ds(512 + i * 128, 128)], here.sibling()
            )
        )

    for i in range(4):
        head_piece(i)
    mark, kept = copies.count, copies.started
    copies.started = []

    @pl.when(core == 0)
    def _():
        run(*[col_ring(part, ("y_first", "z_last")) for part in ((0, 512), (512, 384))])
        copies.finish()

    copies.count = mark

    @pl.when(core == 1)
    def _():
        run(*[col_ring(part, ("z_first", "y_last")) for part in ((0, 512), (512, 384))])
        copies.finish()

    copies.started = kept
    for copy in weights:
        copy.wait()

    def project(k):
        return contract_last(cols[0, :, k].reshape(512, 896), r.weights[0]) + contract_last(
            cols[1, :, k].reshape(512, 896), r.weights[1]
        )

    r.away[...] = project(1 - core).reshape(4, 128, 448)
    swap = copies.go(r.away, r.sib, here.sibling())
    summed = r.summed
    summed[...] = project(core).reshape(4, 128, 448)
    bring(cols, cols_out)
    tgt_wide, mask_wide = r.tgt_wide, r.mask_wide
    mask_rows = []
    for i in range(4):
        at = pl.ds(i * 2 + core, 1)
        tgt_wide[i * 128 : (i + 1) * 128] = spread(targets[at].astype(F32))
        mask_row = loss_mask[at].astype(F32)
        mask_rows.append(mask_row)
        mask_wide[i * 128 : (i + 1) * 128] = spread(mask_row)
    swap.wait_recv()
    for i in range(4):
        summed[i] += r.sib[i]
        r.summed_out[i] = summed[i].astype(BF16)

    def add_x(own, others):
        del own
        total = summed[x]
        for other in others:
            total = total + other[...].astype(F32)
        r.projected[...] = total

    run(reduce_near(copies, here, "x", lambda i: r.summed_out.at[i], r.three, add_x))
    total = r.projected[...]
    piece, pieces = r.piece, r.pieces
    piece[...] = (total * gain[...]).astype(BF16).reshape(piece.shape)
    exchange = []
    for o in range(1, 4):
        to = lax.rem(z + o, 4)
        exchange.append(copies.go(piece.at[to], pieces.at[z], here.along("z", o)))
    pieces[z] = piece[z]
    r.square[...] = lax.dot_general(
        jnp.ones((8, total.shape[1]), F32), total * total, (((1,), (1,)), ((), ())),
        precision=lax.Precision.HIGHEST, preferred_element_type=F32,
    )
    squares, scales = r.squares, r.scales
    squares[here.v] = r.square[...]
    for copy in exchange:
        copy.wait_recv()
    for i in range(4):
        rows[y, x, z, :, i * 448 : (i + 1) * 448] = pieces[i]

    def stage(part, k):
        off, w, order = part

        def slab(i, h):
            index = []
            for a in "yxz":
                at = order.index(a)
                index.append(i if at == k else slice(None) if at < k else here.c[a])
            lines = slice(None) if h is None else pl.ds(h * 16, 16)
            return rows.at[(*index, lines, pl.ds(off, w))]

        ring = gather_near if k < 2 else gather_ring
        return lambda: ring(copies, here, order[k], slab)

    def scale():
        ins = [copies.go(r.square, squares.at[here.v], here.v_peer(o)) for o in range(1, 16)]
        yield
        yield
        for copy in ins:
            copy.wait_recv()
        scales[x] = lax.rsqrt(jnp.sum(squares[...], axis=0) / width + EPSILON)
        ins = [copies.go(scales.at[x], scales.at[x], here.along("x", o)) for o in range(1, 4)]
        yield
        yield
        for copy in ins:
            copy.wait_recv()

    raw = r.raw

    def logits_of(batch):
        off, w = BATCHES[batch]

        @pl.loop(0, 4)
        def _(j):
            term = lax.dot_general(
                rows[j, :, :, :, off : off + w].reshape(512, w),
                head[:, pl.ds(pl.multiple_of(j * 1792 + off, 128), w)],
                (((1,), (1,)), ((), ())), preferred_element_type=F32,
            )
            if batch:
                raw[...] += term
            else:

                @pl.when(j == 0)
                def _():
                    raw[...] = term

                @pl.when(j > 0)
                def _():
                    raw[...] += term

    gathers = [chain(*[stage(part, k) for k in range(3)]) for part in PARTS]
    leading, trailing, scaling = gathers[:3], gathers[3:], scale()

    def advance(group):
        alive = False
        for ring in group:
            try:
                next(ring)
                alive = True
            except StopIteration:
                pass
        return alive

    advance(leading)
    advance([scaling])
    alive = True
    while alive:
        alive = advance(leading)
        advance(trailing)
        advance([scaling])
    while advance([scaling]):
        pass
    load.wait()
    for copy in head_pieces:
        copy.wait_recv()
    logits_of(0)
    advance(trailing)
    logits_of(1)

    scale_wide, log_wide = r.scale_wide, r.log_wide
    for i in range(4):
        scale_wide[i * 128 : (i + 1) * 128] = spread(scales[i, :1])
    column = lax.broadcasted_iota(jnp.int32, (512, 128), 1)
    starts = [(here.ctx * 16 + here.v) * 512, ((here.ctx + 1 - 2 * core) * 16 + here.v) * 512]

    def is_hit(j):
        return tgt_wide[...] == (column + (starts[j // 4] + j % 4 * 128)).astype(F32)

    exps = jnp.zeros((512, 128), F32)
    hits = jnp.zeros((512, 128), F32)
    for j in range(8):
        logit = raw[:, j * 128 : (j + 1) * 128] * scale_wide[...]
        exps = exps + jnp.exp(logit)
        hits = hits + jnp.where(is_hit(j), logit, 0.0)
    tile, sums = r.tile, r.sums
    for i, row in enumerate(lanes(exps) + lanes(hits)):
        tile[i : i + 1] = row
    run(all_sum(copies, here, tile, r.group, r.line, sums))
    logs = jnp.log(sums[:4])
    for i in range(4):
        log_wide[i * 128 : (i + 1) * 128] = spread(logs[i : i + 1])
    grad, grad_t = r.grad, r.grad_t

    def wide_of(j):
        term = raw[:, j * 128 : (j + 1) * 128]
        prob = jnp.exp(term * scale_wide[...] - log_wide[...])
        return mask_wide[...] * (prob - is_hit(j).astype(F32)), term

    for j in range(8):
        grad[:, j * 128 : (j + 1) * 128] = wide_of(j)[0].astype(BF16)
    late = []

    def beside():
        each = logs - sums[4:]
        lost = sum(
            jnp.sum(mask_rows[i] * each[i : i + 1], axis=1, keepdims=True) for i in range(4)
        )
        loss_part = r.loss
        loss_part[core] = jnp.broadcast_to(lost, (8, 128))
        late.append(copies.go(loss_part.at[core], loss_part.at[core], here.sibling()))
        dots = jnp.zeros((512, 128), F32)
        for j in range(8):
            wide, term = wide_of(j)
            dots = dots + wide.astype(BF16).astype(F32) * term
            grad_t[j * 128 : (j + 1) * 128] = (wide * scale_wide[...]).T.astype(BF16)
        dot_tile = r.dot_tile
        for i, row in enumerate(lanes(dots)):
            dot_tile[i : i + 1] = row
            dot_tile[i + 4 : i + 5] = row
        late.append(copies.go(grad_t.at[pl.ds(512, 512)], lgr_sib, here.sibling()))

    terms, whole = r.terms, r.whole

    def half_lines(ref, h):
        index = (slice(None),) * (len(ref.shape) - 2) + (pl.ds(h * 16, 16),)
        return ref.at[index]

    def part_rings(n, part):
        off, w, order = part
        order = order[::-1]
        axes = "yxz"
        cols = pl.ds(off, w)
        one, two, held = r.ones[n], r.twos[n], r.helds[n]
        out = r.outs[n * 2]

        def slab(i, h):
            index = tuple(i if a == order[0] else slice(None) for a in "yxz")
            lines = slice(None) if h is None else pl.ds(h * 16, 16)
            return terms.at[(*index, lines, cols)]

        yield from reduce_ring(copies, here, order[0], slab, half_lines, one, two, held, add_refs)
        add_refs(out, (slab(here.c[order[0]], None), two.at[0], two.at[1]))
        axes = axes.replace(order[0], "")
        last = r.outs[n * 2 + 1]

        def second(i):
            return out.at[tuple(i if a == order[1] else slice(None) for a in axes)]

        yield from reduce_near(
            copies, here, order[1], second, r.threes[n * 2],
            lambda own, others: add_refs(last, (own, *others)),
        )

        def third(own, others):
            total = own[...].astype(F32)
            for other in others:
                total = total + other[...].astype(F32)
            whole[:, off : off + w] = total

        yield from reduce_near(
            copies, here, order[2], lambda i: last.at[i], r.threes[n * 2 + 1], third
        )

    def product(off, w):

        @pl.loop(0, 4)
        def _(j):
            terms[j, :, :, :, off : off + w] = (
                jnp.dot(
                    grad[...], head[:, pl.ds(pl.multiple_of(j * 1792 + off, 128), w)],
                    preferred_element_type=F32,
                )
                .astype(BF16)
                .reshape(4, 4, 32, w)
            )

    swap_rows = []

    def row_piece(j):
        swap_rows.append(copies.go(rows.at[j], rows_sib.at[j], here.sibling()))

    rings = [part_rings(n, part) for n, part in enumerate(PARTS)]
    for n in range(3):
        product(*PARTS[n][:2])
        advance(rings[n : n + 1])
    product(*BATCHES[1])
    advance(rings[3:])
    beside()
    row_dots = all_sum(copies, here, r.dot_tile, r.group2, r.line2, r.sums2)

    def half_head(j):
        lanes_ = pl.ds(j * 1792, 1792)
        head[:512, lanes_] = jnp.dot(
            grad_t[:512], rows[j].reshape(512, 1792), preferred_element_type=F32
        ).astype(BF16)
        bring(head.at[pl.ds(0, 512), lanes_], half_out.at[:, lanes_])

    run(
        *rings,
        row_dots,
        trickle([lambda j=j: row_piece(j) for j in range(4)]),
        trickle([lambda j=j: half_head(j) for j in range(4)]),
    )

    back, backs = r.back, r.backs
    for i in range(4):
        back[i] = whole[:, i * 448 : (i + 1) * 448]
    exchange = []
    for o in range(1, 4):
        to = lax.rem(z + o, 4)
        exchange.append(copies.go(back.at[to], backs.at[z], here.along("z", o)))
    backs[z] = back[z]
    row_scale = scale_wide[pl.ds(pl.multiple_of(x * 128, 128), 128)][:, :1]
    row_dot = spread(r.sums2[pl.ds(x, 1)])[:, :1]
    wide = r.projected[...]
    for copy in exchange:
        copy.wait_recv()
    normed_grad = backs[...].reshape(128, 448)
    grad_out = row_scale * (normed_grad * gain[...]) - wide * (
        row_scale * row_scale * row_scale
    ) * (row_dot / width)
    proj_grad[x, core] = grad_out.astype(BF16)

    def share():
        def at(i):
            return proj_grad.at[i, core]

        def pass_on(i):
            return copies.go(at(i), at(i), here.sibling())

        ins = [copies.go(at(x), at(x), here.along("x", o)) for o in (1, 2, 3)]
        passed = [pass_on(x)]
        yield
        for o in (1, 3, 2):
            ins[o - 1].wait_recv()
            passed.append(pass_on(lax.rem(x + 4 - o, 4)))
        for copy in passed:
            copy.wait_recv()

    def gain_sum():
        mine, every = r.gain_mine, r.gain_all
        mine[...] = jnp.broadcast_to(
            jnp.sum(normed_grad * wide * row_scale, axis=0, keepdims=True), (8, 448)
        )
        every[here.ctx] = mine[...]
        ins = [copies.go(mine, every.at[here.ctx], here.ctx_peer(o)) for o in range(1, 8)]
        yield
        yield
        for copy in ins:
            copy.wait_recv()
        gain_grad[...] = jnp.sum(every[...], axis=0)[:1]

    run(share(), gain_sum())
    for copy in (*swap_rows, *late):
        copy.wait_recv()
    loss[...] = (r.loss[0, :1, :1] + r.loss[1, :1, :1]) / 1024.0
    for copy in locals_[5:]:
        copy.wait()
    copies.finish()


BACK_BATCHES = ((0, 512), (512, 384))


def back_kernel(
    proj_grad, proj_h, proj_e, cols, hidden, embed, gain_h, gain_e, head_half, rows_sib, lgr_sib,
    grad_h, grad_e, gain_grad_h, gain_grad_e, grad_proj_h, grad_proj_e, grad_head,
    r, send, recv, send_far, recv_far, local_sem, out_sem,
):
    r = Bag(r)
    here = Place()
    copies = Copies(send, recv)
    y, z, v, ctx, core = here.c["y"], here.c["z"], here.v, here.ctx, here.core
    width = 7168
    friends = (
        [here.v_peer(o) for o in range(1, 16)]
        + [here.ctx_peer(o) for o in range(1, 8)]
        + [here.at(ctx=v // 2, v=source) for source in range(16)]
    )
    greet(friends)
    locals_ = []

    def bring(src, dst):
        copy = pltpu.make_async_copy(src, dst, local_sem.at[len(locals_)])
        copy.start()
        locals_.append(copy)
        return copy

    weights = [bring(proj_h, r.weights.at[0]), bring(proj_e, r.weights.at[1])]
    cols_in = bring(cols, r.cols)
    inputs = [bring(hidden, r.inputs.at[0]), bring(embed, r.inputs.at[1])]
    lgr_in = bring(lgr_sib, r.lgr)
    rows_in = []
    for j in range(4):
        rows_in.append(
            [
                bring(head_half.at[:, pl.ds(j * 1792, 1792)], r.halves.at[j]),
                bring(rows_sib.at[j], r.rows.at[j]),
            ]
        )
    for copy in weights:
        copy.wait()

    first_at, second_at = jnp.where(core == 0, y, z), jnp.where(core == 0, z, y)

    def near(second, step):
        along_y, along_z = here.along("y", step)["vocab"], here.along("z", step)["vocab"]
        pick = (core == 0) if not second else (core == 1)
        return here.at(v=jnp.where(pick, along_y, along_z))

    ring_first = (first_at, near(False, 1), near(False, -1))
    ring_second = (second_at, [near(True, o) for o in (1, 2, 3)])
    terms, summed, flat = r.terms, r.summed, r.flat

    def fill(batch):
        off, w = BACK_BATCHES[batch]
        for e in range(2):
            back = jnp.dot(
                proj_grad[...], r.weights[e, :, off : off + w], preferred_element_type=F32
            ).astype(BF16)
            flat[e, :, off : off + w] = back
            back = back.reshape(8, 8, 16, w)
            for j in range(8):
                at_y, at_z = e * 2 + j // 4, j % 4
                p = jnp.where(core == 0, at_y, at_z)
                q = jnp.where(core == 0, at_z, at_y)
                terms[p, q, :, :, off : off + w] = back[:, j]

    def back_ring(batch):
        off, w = BACK_BATCHES[batch]
        lanes_ = pl.ds(off, w)

        def span(h):
            return slice(None) if h is None else pl.ds(h * 4, 4)

        one, two, held, out, three = r.rings[batch]

        def big(i, h):
            return terms.at[i, :, span(h), :, lanes_]

        yield from reduce_ring(
            copies, here, ring_first, big, lambda ref, h: ref.at[:, span(h)], one, two, held, add_refs
        )
        add_refs(out, (big(first_at, None), two.at[0], two.at[1]))

        def end(own, others):
            for c in range(8):
                total = own[c].astype(F32)
                for other in others:
                    total = total + other[c].astype(F32)
                summed[c, :, off : off + w] = total

        yield from reduce_near(copies, here, ring_second, lambda i: out.at[i], three, end)

    outs = []

    def head_part(j):
        for copy in rows_in[j]:
            copy.wait()
        slot = j % 2
        if j >= 2:
            outs[j - 2].wait()
        r.stage[slot] = (
            jnp.dot(r.lgr[...], r.rows[j].reshape(512, 1792), preferred_element_type=F32)
            + r.halves[j].astype(F32)
        ).astype(BF16)
        copy = pltpu.make_async_copy(
            r.stage.at[slot], grad_head.at[:, pl.ds(j * 1792, 1792)], out_sem.at[j]
        )
        copy.start()
        outs.append(copy)

    def proj_part(e):
        out = (grad_proj_h, grad_proj_e)[e]
        out[...] = jnp.dot(
            r.turned[...], r.cols[e].reshape(1024, 896), preferred_element_type=F32
        ).astype(BF16)

    mine_dot, dots, dot_rows, dot_in = r.mine_dot, r.dots, r.dot_rows, r.dot_in

    def inner():
        for e in range(2):
            acc = jnp.zeros((1024, 128), F32)
            for c in range(7):
                part = slice(c * 128, (c + 1) * 128)
                cols_part = r.cols[e, :, :, :, :, :, part].reshape(1024, 128).astype(F32)
                acc = acc + flat[e, :, part].astype(F32) * cols_part
            for c in range(8):
                row = jnp.sum(acc[c * 128 : (c + 1) * 128].T, axis=0, keepdims=True)
                mine_dot[e, c : c + 1] = row
        ins = [copies.go(mine_dot, dots.at[v], here.v_peer(o)) for o in range(1, 16)]
        dots[v] = mine_dot[...]
        yield
        for copy in ins:
            copy.wait_recv()
        total = jnp.sum(dots[...], axis=0)
        for c in range(8):
            for e in range(2):
                dot_rows[c, e : e + 1] = total[e, c : c + 1]
        ins = [
            copies.go(dot_rows.at[lax.rem(ctx + o, 8)], dot_in.at[ctx], here.ctx_peer(o))
            for o in range(1, 8)
        ]
        dot_in[ctx] = dot_rows[ctx]
        yield
        for copy in ins:
            copy.wait_recv()

    rings = [back_ring(0), back_ring(1)]
    dotting = inner()
    fill(0)
    met(friends)
    next(rings[0])
    fill(1)
    next(rings[1])
    dot_rows[...] = jnp.zeros_like(dot_rows)
    cols_in.wait()
    next(dotting)
    next(rings[0])
    r.turned[...] = proj_grad[...].astype(F32).T.astype(BF16)
    proj_part(0)
    next(rings[1])
    lgr_in.wait()
    head_part(0)
    head_part(1)
    next(rings[0])
    next(dotting)
    next(rings[1])
    proj_part(1)
    next(rings[0], None)
    next(rings[1], None)
    next(dotting, None)

    sent_gain, got_gain = r.sent_gain, r.got_gain
    gain_acc = jnp.zeros((1, 896), F32)
    for c in range(8):
        gain_acc = gain_acc + jnp.sum(
            summed[c] * r.cols[y // 2, c // 2, c % 2, y % 2, z].astype(F32), axis=0, keepdims=True
        )
    sent_gain[0] = gain_acc[:, :448]
    sent_gain[1] = gain_acc[:, 448:]

    @pl.loop(0, 8)
    def _(c):
        r.sent[0, c] = summed[c][:, :448].astype(BF16)
        r.sent[1, c] = summed[c][:, 448:].astype(BF16)

    sent, got = r.sent, r.got

    def far_copy(o, s):
        to = lax.rem(ctx + o, 8)
        return pltpu.make_async_remote_copy(
            src_ref=sent.at[s, to],
            dst_ref=got.at[v // 8, pl.ds(pl.multiple_of(lax.rem(v, 8) * 16, 16), 16)],
            send_sem=send_far.at[o * 2 + s],
            recv_sem=recv_far.at[v],
            device_id=here.at(ctx=to, v=ctx * 2 + s),
            device_id_type=MESH,
        )

    def far_gain(o, s):
        return pltpu.make_async_remote_copy(
            src_ref=sent_gain.at[s],
            dst_ref=got_gain.at[v],
            send_sem=send_far.at[16 + o * 2 + s],
            recv_sem=recv_far.at[16 + v],
            device_id=here.at(ctx=lax.rem(ctx + o, 8), v=ctx * 2 + s),
            device_id_type=MESH,
        )

    for o in range(8):
        for s in range(2):
            if o:
                far_copy(o, s).start()
                far_gain(o, s).start()
            else:

                @pl.when(v != ctx * 2 + s)
                def _(s=s):
                    far_copy(0, s).start()
                    far_gain(0, s).start()

                @pl.when(v == ctx * 2 + s)
                def _(s=s):
                    got_gain[v] = sent_gain[s]
                    got[v // 8, pl.ds(pl.multiple_of(lax.rem(v, 8) * 16, 16), 16)] = sent[s, ctx]

    for copy in inputs:
        copy.wait()
    odd = lax.rem(v, 2)
    window = pl.ds(pl.multiple_of(v // 2 * 896 + odd * 384, 128), 512)
    mine, gains, scales = r.mine, r.gains, r.scales
    for e, gain in enumerate((gain_h, gain_e)):
        squares = jnp.zeros((128, 128), F32)
        for c in range(56):
            part = r.inputs[e, :, c * 128 : (c + 1) * 128].astype(F32)
            squares = squares + part * part
        scales[e] = jnp.broadcast_to(
            lax.rsqrt(jnp.sum(squares, axis=1, keepdims=True) / width + EPSILON), (128, 128)
        )

        @pl.when(odd == 0)
        def _(e=e, gain=gain):
            mine[e] = r.inputs[e, :, window][:, :448].astype(F32)
            gains[e] = gain[:, window][:, :448]

        @pl.when(odd == 1)
        def _(e=e, gain=gain):
            mine[e] = r.inputs[e, :, window].astype(F32)[:, 64:]
            gains[e] = gain[:, window][:, 64:]

    head_part(2)
    head_part(3)
    for source in range(16):

        @pl.when(jnp.logical_or(ctx != v // 2, v != source))
        def _(source=source):
            pltpu.make_async_remote_copy(
                src_ref=sent.at[0, 0],
                dst_ref=got.at[source // 8, pl.ds(source % 8 * 16, 16)],
                send_sem=send_far.at[0],
                recv_sem=recv_far.at[source],
                device_id=here.at(ctx=lax.rem(ctx + 1, 8)),
                device_id_type=MESH,
            ).wait_recv()
            pltpu.make_async_remote_copy(
                src_ref=sent_gain.at[0],
                dst_ref=got_gain.at[source],
                send_sem=send_far.at[0],
                recv_sem=recv_far.at[16 + source],
                device_id=here.at(ctx=lax.rem(ctx + 1, 8)),
                device_id_type=MESH,
            ).wait_recv()

    dot_sum = jnp.sum(dot_in[...], axis=0).T
    for e, (out, gain_out) in enumerate(((grad_h, gain_grad_h), (grad_e, gain_grad_e))):
        back = got[e].astype(F32)
        scale = scales[e][:, :1]
        dot = dot_sum[:, e : e + 1]
        grad = scale * (back * gains[e]) - mine[e] * (scale * scale) * (dot / width)
        out[...] = grad.T.astype(BF16)
        gain_out[...] = jnp.sum(got_gain[e * 8 : e * 8 + 8], axis=0) / gains[e]
    for o in range(8):
        for s in range(2):
            if o:
                far_copy(o, s).wait_send()
                far_gain(o, s).wait_send()
            else:

                @pl.when(v != ctx * 2 + s)
                def _(s=s):
                    far_copy(0, s).wait_send()
                    far_gain(0, s).wait_send()

    for copy in outs[2:]:
        copy.wait()
    copies.finish()


def place_kernel(*refs):
    ins, outs, buffers, sem_in, sem_out = refs[:9], refs[9:18], refs[18:23], refs[23], refs[24]
    moves = [(ins[4 + i], buffers[i], outs[4 + i]) for i in range(4)]
    for i in range(8):
        lines = pl.ds(i * 64, 64)
        moves.append((ins[8].at[lines], buffers[4].at[lines], outs[8].at[lines]))
    loads = [pltpu.make_async_copy(a, b, sem_in.at[n]) for n, (a, b, _) in enumerate(moves)]
    stores = [pltpu.make_async_copy(b, c, sem_out.at[n]) for n, (_, b, c) in enumerate(moves)]
    for load in loads:
        load.start()
    for value, out in zip(ins[:4], outs[:4]):
        out[...] = value[...]
    for load, store in zip(loads, stores):
        load.wait()
        store.start()
    for store in stores:
        store.wait()


def back_scratch():
    scratch = dict(
        weights=pltpu.VMEM((2, 448, 896), BF16),
        cols=pltpu.VMEM((2, 4, 2, 2, 4, 16, 896), BF16),
        inputs=pltpu.VMEM((2, 128, 7168), BF16),
        lgr=pltpu.VMEM((512, 512), BF16),
        rows=pltpu.VMEM((4, 4, 4, 32, 1792), BF16),
        halves=pltpu.VMEM((4, 512, 1792), BF16),
        terms=pltpu.VMEM((4, 4, 8, 16, 896), BF16),
        summed=pltpu.VMEM((8, 16, 896), F32),
        stage=pltpu.VMEM((2, 512, 1792), BF16),
        turned=pltpu.VMEM((448, 1024), BF16),
        sent=pltpu.VMEM((2, 8, 16, 448), BF16),
        got=pltpu.VMEM((2, 128, 448), BF16),
        mine=pltpu.VMEM((2, 128, 448), F32),
        gains=pltpu.VMEM((2, 1, 448), F32),
        scales=pltpu.VMEM((2, 128, 128), F32),
        mine_dot=pltpu.VMEM((2, 8, 128), F32),
        dots=pltpu.VMEM((16, 2, 8, 128), F32),
        dot_rows=pltpu.VMEM((8, 8, 128), F32),
        dot_in=pltpu.VMEM((8, 8, 128), F32),
        sent_gain=pltpu.VMEM((2, 1, 448), F32),
        got_gain=pltpu.VMEM((16, 1, 448), F32),
        flat=pltpu.VMEM((2, 1024, 896), BF16),
        rings=[],
    )
    for n, (_, w) in enumerate(BACK_BATCHES):
        scratch["rings"].append(
            [
                pltpu.VMEM((2, 4, 4, 16, w), BF16),
                pltpu.VMEM((2, 4, 8, 16, w), BF16),
                pltpu.VMEM((2, 4, 4, 16, w), BF16),
                pltpu.VMEM((4, 8, 16, w), BF16),
                pltpu.VMEM((3, 8, 16, w), BF16),
            ]
        )
    return scratch


def params(number, limit=56):
    return pltpu.CompilerParams(
        collective_id=number, has_side_effects=True, vmem_limit_bytes=limit * 2**20
    )


def sems(n):
    return [pltpu.SemaphoreType.DMA((n,)), pltpu.SemaphoreType.DMA((n,))]


def shape(dims, kind):
    return jax.ShapeDtypeStruct(dims, kind)


def middle_scratch():
    scratch = dict(
        head=pltpu.VMEM((1024, 7168), BF16),
        rows=pltpu.VMEM((4, 4, 4, 32, 1792), BF16),
        terms=pltpu.VMEM((4, 4, 4, 32, 1792), BF16),
        raw=pltpu.VMEM((512, 1024), F32),
        grad=pltpu.VMEM((512, 1024), BF16),
        grad_t=pltpu.VMEM((1024, 512), BF16),
        scale_wide=pltpu.VMEM((512, 128), F32),
        log_wide=pltpu.VMEM((512, 128), F32),
        cols=pltpu.VMEM((2, 4, 2, 2, 4, 16, 896), BF16),
        raw_in=pltpu.VMEM((2, 16, 7168), BF16),
        normed=pltpu.VMEM((8, 16, 896), BF16),
        weights=pltpu.VMEM((2, 448, 896), BF16),
        loss=pltpu.VMEM((2, 8, 128), F32),
        tgt_wide=pltpu.VMEM((512, 128), F32),
        mask_wide=pltpu.VMEM((512, 128), F32),
        away=pltpu.VMEM((4, 128, 448), F32),
        sib=pltpu.VMEM((4, 128, 448), F32),
        summed=pltpu.VMEM((4, 128, 448), F32),
        summed_out=pltpu.VMEM((4, 128, 448), BF16),
        three=pltpu.VMEM((3, 128, 448), BF16),
        projected=pltpu.VMEM((128, 448), F32),
        square=pltpu.VMEM((8, 128), F32),
        squares=pltpu.VMEM((16, 8, 128), F32),
        scales=pltpu.VMEM((4, 8, 128), F32),
        piece=pltpu.VMEM((4, 32, 448), BF16),
        pieces=pltpu.VMEM((4, 32, 448), BF16),
        back=pltpu.VMEM((4, 32, 448), F32),
        backs=pltpu.VMEM((4, 32, 448), F32),
        whole=pltpu.VMEM((32, 1792), F32),
        gain_mine=pltpu.VMEM((8, 448), F32),
        gain_all=pltpu.VMEM((8, 8, 448), F32),
        tile=pltpu.VMEM((8, 128), F32),
        sums=pltpu.VMEM((8, 128), F32),
        dot_tile=pltpu.VMEM((8, 128), F32),
        sums2=pltpu.VMEM((8, 128), F32),
        group=pltpu.VMEM((16, 8, 128), F32),
        group2=pltpu.VMEM((16, 8, 128), F32),
        line=pltpu.VMEM((4, 8, 128), F32),
        line2=pltpu.VMEM((4, 8, 128), F32),
        ones=[],
        threes=[],
        twos=[],
        helds=[],
        outs=[],
    )
    for _, w, _ in PARTS:
        scratch["ones"].append(pltpu.VMEM((2, 4, 4, 16, w), BF16))
        scratch["helds"].append(pltpu.VMEM((2, 4, 4, 16, w), BF16))
        scratch["twos"].append(pltpu.VMEM((2, 4, 4, 32, w), BF16))
        scratch["outs"] += [pltpu.VMEM((4, 4, 32, w), BF16), pltpu.VMEM((4, 32, w), BF16)]
        scratch["threes"] += [pltpu.VMEM((3, 4, 32, w), BF16), pltpu.VMEM((3, 32, w), BF16)]
    return scratch


def contract_last(left, right):
    return lax.dot_general(
        left, right, (((1,), (1,)), ((), ())), preferred_element_type=F32
    )


def local(
    hidden_state, embedded_next, gain_hidden, gain_embed, proj_hidden, proj_embed,
    final_gain, head, targets, loss_mask,
):
    proj_grad, gain_grad, loss, cols, head_half, rows_sib, lgr_sib = pl.pallas_call(
        middle_kernel,
        out_shape=[
            shape((4, 2, 128, 448), BF16), shape((1, 448), F32), shape((1, 1), F32),
            shape((2, 4, 2, 2, 4, 16, 896), BF16),
            shape(head.shape, BF16), shape((4, 4, 4, 32, 1792), BF16), shape((512, 512), BF16),
        ],
        in_specs=[ANY, ANY, VMEM, VMEM, ANY, ANY, VMEM, ANY, VMEM, VMEM],
        out_specs=[VMEM, VMEM, VMEM, ANY, ANY, ANY, ANY],
        scratch_shapes=[middle_scratch()] + sems(360) + [pltpu.SemaphoreType.DMA((10,))],
        compiler_params=params(2, 61),
        name="middle",
    )(
        hidden_state, embedded_next, gain_hidden[None, :], gain_embed[None, :],
        proj_hidden.T, proj_embed.T, final_gain[None, :], head,
        targets.reshape(8, 128), loss_mask.reshape(8, 128),
    )
    grad_h, grad_e, gain_grad_h, gain_grad_e, grad_proj_h, grad_proj_e, grad_head = pl.pallas_call(
        back_kernel,
        out_shape=[
            shape((448, 128), BF16), shape((448, 128), BF16), shape((1, 448), F32), shape((1, 448), F32),
            shape((448, 896), BF16), shape((448, 896), BF16), shape(head.shape, BF16),
        ],
        in_specs=[VMEM, ANY, ANY, ANY, ANY, ANY, VMEM, VMEM, ANY, ANY, ANY],
        out_specs=[VMEM] * 6 + [ANY],
        scratch_shapes=[back_scratch()]
        + sems(46)
        + sems(32)
        + [pltpu.SemaphoreType.DMA((15,)), pltpu.SemaphoreType.DMA((4,))],
        compiler_params=params(5, 58),
        name="back",
    )(
        proj_grad.reshape(1024, 448), proj_hidden.T, proj_embed.T, cols, hidden_state, embedded_next,
        gain_hidden[None, :], gain_embed[None, :], head_half, rows_sib, lgr_sib,
    )
    values = [
        loss, gain_grad_h, gain_grad_e, gain_grad, grad_h, grad_e, grad_proj_h, grad_proj_e, grad_head,
    ]
    specs = [VMEM] * 4 + [ANY] * 5
    loss, gain_grad_h, gain_grad_e, gain_grad, grad_h, grad_e, grad_proj_h, grad_proj_e, grad_head = (
        pl.pallas_call(
            place_kernel,
            out_shape=[shape(value.shape, value.dtype) for value in values],
            in_specs=specs,
            out_specs=specs,
            scratch_shapes=[pltpu.VMEM(value.shape, value.dtype) for value in values[4:]]
            + [pltpu.SemaphoreType.DMA((12,)), pltpu.SemaphoreType.DMA((12,))],
            compiler_params=pltpu.CompilerParams(vmem_limit_bytes=60 * 2**20),
            name="place",
        )(*values)
    )
    return (
        loss[0, 0], grad_h.T, grad_e.T, gain_grad_h[0], gain_grad_e[0],
        grad_proj_h.T, grad_proj_e.T, gain_grad[0], grad_head,
    )


def solution(mesh):
    in_specs = (
        P("ctx", None), P("ctx", None), P(), P(), P("ctx", "vocab"), P("ctx", "vocab"),
        P("vocab"), P(("ctx", "vocab"), None), P(), P(),
    )
    out_specs = (
        P(), P("ctx", "vocab"), P("ctx", "vocab"), P("vocab"), P("vocab"),
        P("ctx", "vocab"), P("ctx", "vocab"), P("vocab"), P(("ctx", "vocab"), None),
    )
    return jax.shard_map(local, mesh=mesh, in_specs=in_specs, out_specs=out_specs, check_vma=False)
```

time: 293 us -> 216 us (0.74)
  Pallas kernels: 251 us -> 214 us
  local copies, waits for them, and re-layouts: 16.9 us -> 0 us
  other arithmetic: 10.6 us -> 0 us
  matrix products: 10.2 us -> 0 us
    pallas_call x3 -> x2, Pallas kernels: 106 us -> 49.7 us  [the longest x1 40.7 us: local(): pl.pallas_call(back_kernel, out_shape=[shape((448, 128), BF16), shape((44...]
    pallas_call x1, Pallas kernels: 145 us -> 165 us  [local(): pl.pallas_call(middle_kernel, out_shape=[shape((4, 2, 128, 448), BF16), s...]
    dot_general x6 -> x0, matrix products: 10.2 us -> none  [the longest x2 4.09 us: contract_first(): lax.dot_general(left, right, (((0,), (0,)), ((), ())), preferred_element_...]
    slice x3 -> x0, local copies, waits for them, and re-layouts: 4.97 us -> none  [the longest x1 2.46 us: local(): embed_cols = cols[1].reshape(1024, 896)]
    reduce_sum x3 -> x0, other arithmetic: 3.68 us -> none  [scale_of(): jnp.mean(values * values, axis=-1, keepdims=True) + EPSILON]
    another operation x4 -> x0, other arithmetic: 3.59 us -> none  [the longest x1 2.17 us: local(): jnp.stack([contract_last(proj_grad, proj_hidden).astype(BF16), contract_l...]
where the time goes in v3:
time: 216 us; the launch traced here: 215 us
  Pallas kernels  214 us (99%)
    pallas_call x1, Pallas kernels, local(): pl.pallas_call(middle_kernel, out_shape=[shape((4, 2, 128, 448), BF16), s...  165 us
    pallas_call x1, Pallas kernels, local(): pl.pallas_call(back_kernel, out_shape=[shape((448, 128), BF16), shape((44...  40.7 us
    pallas_call x1, Pallas kernels, local(): pl.pallas_call(place_kernel, out_shape=[shape(value.shape, value.dtype) f...  9.01 us

profile of v3, /device:TPU:1, one launch (start us, length us, event | category | flops | bytes accessed | tf_op | source)
XLA Modules:
  0.0 215.3 jit_solution(379427351710094059)
XLA Ops:
  0.6 164.7 %middle.1 = (bf16[4,2,128,448]{3,2,1,0:T(8,128)(2,1)}, f32[1,448]{1,0:T(1,128)}, f32[1,1]{1,0:T(1,128)}, bf16[2,4,2,2,4,16,896]{6,5,4,3,2,1,0:T(8,128)(2,1)}, bf...) custom-call(bf16[128,7168]{1,0:T(8,128)(2,1)} %hidden.3, ...), custom_call_target="tpu_custom_call" | custom-call | tf_op jit(solution)/shard_map/middle/pallas_call | solution.py:1099
  165.4 40.7 %back.1 = (bf16[448,128]{1,0:T(8,128)(2,1)}, bf16[448,128]{1,0:T(8,128)(2,1)}, f32[1,448]{1,0:T(1,128)}, f32[1,448]{1,0:T(1,128)}, bf16[448,896]{1,0:T(8,128)(2,...) custom-call(bf16[1024,448]{1,0:T(8,128)(2,1)} %bitcast.20, bf16[448,896]{1,0:T(8,128)(2,1)} %bitcast.17, ...), custom_call_target="tpu_custom_call" | custom-call | tf_op jit(solution)/shard_map/back/pallas_call | solution.py:1116
  206.1 9.0 %place.1 = (f32[1,1]{1,0:T(1,128)}, f32[1,448]{1,0:T(1,128)}, f32[1,448]{1,0:T(1,128)}, f32[1,448]{1,0:T(1,128)}, bf16[448,128]{1,0:T(8,128)(2,1)}, /*index=5*/b...) custom-call(f32[1,1]{1,0:T(1,128)} %get-tuple-element.32.refs_0_, ...), custom_call_target="tpu_custom_call" | custom-call | tf_op jit(solution)/shard_map/place/pallas_call | solution.py:1139

commit v4 on v3

--- a/solution.py
+++ b/solution.py
@@ -20,6 +20,7 @@
     (1536, 256, "zxy"),
 )
 BATCHES = ((0, 1024), (1024, 768))
+SHARED = 640
 
 
 class Place:
@@ -252,8 +253,8 @@
 
     sliver = pl.ds(pl.multiple_of(lax.rem(here.v, 8) * 16, 16), 16)
     raw_in = [bring(hidden.at[sliver], r.raw_in.at[0]), bring(embed.at[sliver], r.raw_in.at[1])]
+    wide_in = [bring(hidden, head.at[pl.ds(0, 128)]), bring(embed, head.at[pl.ds(128, 128)])]
     weights = [bring(proj_h, r.weights.at[0]), bring(proj_e, r.weights.at[1])]
-    load = bring(head_own, head.at[pl.ds(0, 512)])
     for copy in raw_in:
         copy.wait()
     first = here.v < 8
@@ -263,7 +264,7 @@
         wide = r.raw_in[e].astype(F32)
         scale = lax.rsqrt(jnp.mean(wide * wide, axis=-1, keepdims=True) + EPSILON)
         for c in range(8):
-            part = slice(c * 896, (c + 1) * 896)
+            part = slice(c * 896, c * 896 + SHARED)
             normed[c] = (wide[:, part] * scale * gains[:, part]).astype(BF16)
 
     @pl.when(first)
@@ -277,13 +278,14 @@
     met(friends)
 
     def sliver_at(c):
-        return cols.at[y // 2, c // 2, c % 2, y % 2, z]
+        return cols.at[y // 2, c // 2, c % 2, y % 2, z, :, pl.ds(0, SHARED)]
 
     arrivals = []
     for o in range(1, 8):
         peer = lax.rem(here.ctx + o, 8)
         arrivals.append(copies.go(normed.at[peer], sliver_at(here.ctx), here.ctx_peer(o)))
-    cols[y // 2, x, core, y % 2, z] = normed[here.ctx]
+    cols[y // 2, x, core, y % 2, z, :, :SHARED] = normed[here.ctx]
+
     for arrival in arrivals:
         arrival.wait_recv()
 
@@ -307,6 +309,41 @@
             lambda: gather_ring(copies, here, names[1][0], slabs[names[1]]),
         )
 
+    def straight_part():
+        direct = r.direct
+        for copy in wide_in:
+            copy.wait()
+        for e, gains in enumerate((gain_h, gain_e)):
+            lines = slice(e * 128, (e + 1) * 128)
+            squares = jnp.zeros((128, 128), F32)
+            for c in range(56):
+                part = head[lines, c * 128 : (c + 1) * 128].astype(F32)
+                squares = squares + part * part
+            scale = lax.rsqrt(jnp.sum(squares, axis=1, keepdims=True) / width + EPSILON)
+            for c in range(8):
+                part = slice(c * 896 + SHARED, (c + 1) * 896)
+                direct[c, e] = (
+                    (head[lines, part].astype(F32) * scale * gains[:, part])
+                    .astype(BF16)
+                    .reshape(2, 4, 16, 896 - SHARED)
+                )
+
+        straight = []
+        for o in range(1, 8):
+            peer = lax.rem(here.ctx + o, 8)
+            straight.append(
+                copies.go(
+                    direct.at[peer],
+                    cols.at[:, x, core, :, :, :, pl.ds(SHARED, 896 - SHARED)],
+                    here.ctx_peer(o),
+                )
+            )
+        cols[:, x, core, :, :, :, SHARED:] = direct[here.ctx]
+        yield
+        yield
+        for copy in straight:
+            copy.wait_recv()
+
     head_pieces = []
 
     def head_piece(i):
@@ -324,17 +361,18 @@
 
     @pl.when(core == 0)
     def _():
-        run(*[col_ring(part, ("y_first", "z_last")) for part in ((0, 512), (512, 384))])
+        run(*[col_ring(part, ("y_first", "z_last")) for part in ((0, 384), (384, 256))], straight_part())
         copies.finish()
 
     copies.count = mark
 
     @pl.when(core == 1)
     def _():
-        run(*[col_ring(part, ("z_first", "y_last")) for part in ((0, 512), (512, 384))])
+        run(*[col_ring(part, ("z_first", "y_last")) for part in ((0, 384), (384, 256))], straight_part())
         copies.finish()
 
     copies.started = kept
+    loads = [bring(head_own.at[pl.ds(i * 128, 128)], head.at[pl.ds(i * 128, 128)]) for i in range(4)]
     for copy in weights:
         copy.wait()
 
@@ -461,7 +499,8 @@
         advance([scaling])
     while advance([scaling]):
         pass
-    load.wait()
+    for copy in loads:
+        copy.wait()
     for copy in head_pieces:
         copy.wait_recv()
     logits_of(0)
@@ -655,7 +694,7 @@
     for copy in (*swap_rows, *late):
         copy.wait_recv()
     loss[...] = (r.loss[0, :1, :1] + r.loss[1, :1, :1]) / 1024.0
-    for copy in locals_[5:]:
+    for copy in [copy for copy in locals_[6:] if not any(copy is one for one in loads)]:
         copy.wait()
     copies.finish()
 
@@ -1042,7 +1081,8 @@
         log_wide=pltpu.VMEM((512, 128), F32),
         cols=pltpu.VMEM((2, 4, 2, 2, 4, 16, 896), BF16),
         raw_in=pltpu.VMEM((2, 16, 7168), BF16),
-        normed=pltpu.VMEM((8, 16, 896), BF16),
+        normed=pltpu.VMEM((8, 16, SHARED), BF16),
+        direct=pltpu.VMEM((8, 2, 2, 4, 16, 896 - SHARED), BF16),
         weights=pltpu.VMEM((2, 448, 896), BF16),
         loss=pltpu.VMEM((2, 8, 128), F32),
         tgt_wide=pltpu.VMEM((512, 128), F32),
@@ -1105,7 +1145,7 @@
         ],
         in_specs=[ANY, ANY, VMEM, VMEM, ANY, ANY, VMEM, ANY, VMEM, VMEM],
         out_specs=[VMEM, VMEM, VMEM, ANY, ANY, ANY, ANY],
-        scratch_shapes=[middle_scratch()] + sems(360) + [pltpu.SemaphoreType.DMA((10,))],
+        scratch_shapes=[middle_scratch()] + sems(360) + [pltpu.SemaphoreType.DMA((16,))],
         compiler_params=params(2, 61),
         name="middle",
     )(

time: 216 us -> 212 us (0.981)
  Pallas kernels: 214 us -> 210 us
    pallas_call x1, Pallas kernels: 165 us -> 161 us  [local(): pl.pallas_call(middle_kernel, out_shape=[shape((4, 2, 128, 448), BF16), s...]
where the time goes in v4:
time: 212 us; the launch traced here: 211 us
  Pallas kernels  210 us (99%)
    pallas_call x1, Pallas kernels, local(): pl.pallas_call(middle_kernel, out_shape=[shape((4, 2, 128, 448), BF16), s...  161 us
    pallas_call x1, Pallas kernels, local(): pl.pallas_call(back_kernel, out_shape=[shape((448, 128), BF16), shape((44...  40 us
    pallas_call x1, Pallas kernels, local(): pl.pallas_call(place_kernel, out_shape=[shape(value.shape, value.dtype) f...  9.01 us

profile of v4, /device:TPU:1, one launch (start us, length us, event | category | flops | bytes accessed | tf_op | source)
XLA Modules:
  0.0 210.6 jit_solution(10809783418339189641)
XLA Ops:
  0.6 160.7 %middle.1 = (bf16[4,2,128,448]{3,2,1,0:T(8,128)(2,1)}, f32[1,448]{1,0:T(1,128)}, f32[1,1]{1,0:T(1,128)}, bf16[2,4,2,2,4,16,896]{6,5,4,3,2,1,0:T(8,128)(2,1)}, bf...) custom-call(bf16[128,7168]{1,0:T(8,128)(2,1)} %hidden.3, ...), custom_call_target="tpu_custom_call" | custom-call | tf_op jit(solution)/shard_map/middle/pallas_call | solution.py:1139
  161.4 40.0 %back.1 = (bf16[448,128]{1,0:T(8,128)(2,1)}, bf16[448,128]{1,0:T(8,128)(2,1)}, f32[1,448]{1,0:T(1,128)}, f32[1,448]{1,0:T(1,128)}, bf16[448,896]{1,0:T(8,128)(2,...) custom-call(bf16[1024,448]{1,0:T(8,128)(2,1)} %bitcast.20, bf16[448,896]{1,0:T(8,128)(2,1)} %bitcast.17, ...), custom_call_target="tpu_custom_call" | custom-call | tf_op jit(solution)/shard_map/back/pallas_call | solution.py:1156
  201.4 9.0 %place.1 = (f32[1,1]{1,0:T(1,128)}, f32[1,448]{1,0:T(1,128)}, f32[1,448]{1,0:T(1,128)}, f32[1,448]{1,0:T(1,128)}, bf16[448,128]{1,0:T(8,128)(2,1)}, /*index=5*/b...) custom-call(f32[1,1]{1,0:T(1,128)} %get-tuple-element.32.refs_0_, ...), custom_call_target="tpu_custom_call" | custom-call | tf_op jit(solution)/shard_map/place/pallas_call | solution.py:1179

commit v5 on v4

--- a/solution.py
+++ b/solution.py
@@ -699,7 +699,7 @@
     copies.finish()
 
 
-BACK_BATCHES = ((0, 512), (512, 384))
+BACK_BATCHES = ((0, 384), (384, 512))
 
 
 def back_kernel(
@@ -1000,8 +1000,8 @@
 def place_kernel(*refs):
     ins, outs, buffers, sem_in, sem_out = refs[:9], refs[9:18], refs[18:23], refs[23], refs[24]
     moves = [(ins[4 + i], buffers[i], outs[4 + i]) for i in range(4)]
-    for i in range(8):
-        lines = pl.ds(i * 64, 64)
+    for i in range(16):
+        lines = pl.ds(i * 32, 32)
         moves.append((ins[8].at[lines], buffers[4].at[lines], outs[8].at[lines]))
     loads = [pltpu.make_async_copy(a, b, sem_in.at[n]) for n, (a, b, _) in enumerate(moves)]
     stores = [pltpu.make_async_copy(b, c, sem_out.at[n]) for n, (_, b, c) in enumerate(moves)]
@@ -1182,7 +1182,7 @@
             in_specs=specs,
             out_specs=specs,
             scratch_shapes=[pltpu.VMEM(value.shape, value.dtype) for value in values[4:]]
-            + [pltpu.SemaphoreType.DMA((12,)), pltpu.SemaphoreType.DMA((12,))],
+            + [pltpu.SemaphoreType.DMA((20,)), pltpu.SemaphoreType.DMA((20,))],
             compiler_params=pltpu.CompilerParams(vmem_limit_bytes=60 * 2**20),
             name="place",
         )(*values)

time: 212 us -> 218 us (1.028)
  the two profiles are of different devices: /device:TPU:1 before, /device:TPU:17 now
where the time goes in v5:
time: 218 us
  Pallas kernels  217 us (100%)
    pallas_call x1, Pallas kernels, local(): pl.pallas_call(middle_kernel, out_shape=[shape((4, 2, 128, 448), BF16), s...  158 us
    pallas_call x1, Pallas kernels, local(): pl.pallas_call(back_kernel, out_shape=[shape((448, 128), BF16), shape((44...  49.7 us
    pallas_call x1, Pallas kernels, local(): pl.pallas_call(place_kernel, out_shape=[shape(value.shape, value.dtype) f...  9.08 us

profile of v5, /device:TPU:17, one launch (start us, length us, event | category | flops | bytes accessed | tf_op | source)
XLA Modules:
  0.0 217.8 jit_solution(2903149522084038267)
XLA Ops:
  0.6 158.2 %middle.1 = (bf16[4,2,128,448]{3,2,1,0:T(8,128)(2,1)}, f32[1,448]{1,0:T(1,128)}, f32[1,1]{1,0:T(1,128)}, bf16[2,4,2,2,4,16,896]{6,5,4,3,2,1,0:T(8,128)(2,1)}, bf...) custom-call(bf16[128,7168]{1,0:T(8,128)(2,1)} %hidden.3, ...), custom_call_target="tpu_custom_call" | custom-call | tf_op jit(solution)/shard_map/middle/pallas_call | solution.py:1139
  158.9 49.7 %back.1 = (bf16[448,128]{1,0:T(8,128)(2,1)}, bf16[448,128]{1,0:T(8,128)(2,1)}, f32[1,448]{1,0:T(1,128)}, f32[1,448]{1,0:T(1,128)}, bf16[448,896]{1,0:T(8,128)(2,...) custom-call(bf16[1024,448]{1,0:T(8,128)(2,1)} %bitcast.20, bf16[448,896]{1,0:T(8,128)(2,1)} %bitcast.17, ...), custom_call_target="tpu_custom_call" | custom-call | tf_op jit(solution)/shard_map/back/pallas_call | solution.py:1156
  208.5 9.1 %place.1 = (f32[1,1]{1,0:T(1,128)}, f32[1,448]{1,0:T(1,128)}, f32[1,448]{1,0:T(1,128)}, f32[1,448]{1,0:T(1,128)}, bf16[448,128]{1,0:T(8,128)(2,1)}, /*index=5*/b...) custom-call(f32[1,1]{1,0:T(1,128)} %get-tuple-element.32.refs_0_, ...), custom_call_target="tpu_custom_call" | custom-call | tf_op jit(solution)/shard_map/place/pallas_call | solution.py:1179
